TPU v7x, 32 devices: a whole 2x2x4 slice. The times are simulated.
32 devices in a mesh: grp: 2 (over x), rows: 16 (over z, y, core).
Axes of the slice: x: 2, y: 2, z: 4, core: 2. Of those that a mesh axis runs over, the one named last changes fastest.
Arguments:
- histories: float32 [4096, 384], P(('grp', 'rows')), parts along dimension 0, may hold values from -6 to 6
- modal_map: float32 [4096, 8192], P(('grp', 'rows')), parts along dimension 0, may hold values from -0.1875 to 0.1875
- recovery: float32 [8192, 8192], P(('grp', 'rows')), parts along dimension 0, may hold values from -0.0625 to 0.0625
Outputs:
- responses: float32 [8192, 384], P(('grp', 'rows')), parts along dimension 0
- peak_response: float32 [4, 8192], P(None, ('grp', 'rows')), parts along dimension 1
- rms_response: float32 [4, 8192], P(None, ('grp', 'rows')), parts along dimension 1
There are 2 independent parts, one for each index of `grp`. A program takes and returns all parts, laid end to end along the dimension named above; each array names one. Nothing has to cross between parts.
All inputs are finite; a program needn't handle non-finite values.
Results may differ from a plain program's by a relative error of at most 0.000071.
Values sent between devices are 32-bit elements; how exact they have to be, the bound alone decides.
No kernel may reach another device: no remote copies, remote signals or barrier semaphores. Data moves between devices by JAX's collectives and lax.ppermute only.
A program may use at most 64 MiB of HBM per device.

v0:
```python
import jax
import jax.numpy as jnp
from jax import lax
from jax.sharding import PartitionSpec as P

CASES = 4


epsilon = 1e-06


def shards(histories, modal_map, recovery):
    time_cols = histories.shape[1]
    modal_rows = lax.psum_scatter(
        lax.dot_general(
            modal_map,
            histories,
            (((0,), (0,)), ((), ())),
            precision=lax.Precision.HIGHEST,
            preferred_element_type=jnp.float32,
        ),
        "rows",
        scatter_dimension=0,
        tiled=True,
    )
    responses = jnp.dot(
        recovery,
        lax.all_gather(modal_rows, "rows", axis=0, tiled=True),
        precision=lax.Precision.HIGHEST,
        preferred_element_type=jnp.float32,
    )
    by_case = responses.reshape(responses.shape[0], CASES, time_cols // CASES)
    peak_response = jnp.max(jnp.abs(by_case), axis=2).T
    rms_response = jnp.sqrt(jnp.mean(by_case * by_case, axis=2) + epsilon).T
    return (responses, peak_response, rms_response)


def solution(mesh):
    return jax.shard_map(
        shards,
        mesh=mesh,
        in_specs=(P(("grp", "rows"), None), P(("grp", "rows"), None), P(("grp", "rows"), None)),
        out_specs=(P(("grp", "rows"), None), P(None, ("grp", "rows")), P(None, ("grp", "rows"))),
        check_vma=False,
    )
```

profile of v0, /device:TPU:0, one launch (start us, length us, event | category | flops | bytes accessed | tf_op | source)
XLA Modules:
  0.0 294.4 jit_solution(7221013684479145059)
XLA Ops:
  7.2 0.0 copy-start
  7.2 0.0 reduce-scatter.2.cloned.1.call-start
  7.2 0.9 copy-done
  8.1 13.6 %fusion.1 = f32[8192,384]{1,0:T(8,128)} fusion(f32[128,8192]{1,0:T(8,128)} %param.4, f32[128,384]{1,0:T(8,128)S(1)} %copy-done), kind=kOutput, calls=%fused_computation.3 | convolution fusion | flops 4831838208 | bytes 16973824 | tf_op jit(solution)/shard_map/dot_general | solution.py:15
  21.7 0.0 reduce-scatter.2.cloned.1.call-update
  21.7 0.2 all-gather.2.cloned.1.call-start
  21.9 137.2 %reduce-scatter.2.cloned.1.call-done = f32[512,384]{1,0:T(8,128)} async-done(((f32[8192,384]{1,0:T(8,128)}), f32[512,384]{1,0:T(8,128)}) %reduce-scatter.2.cloned.1.call-update) | async-done | bytes 786448 | tf_op jit(solution)/shard_map/reduce_scatter | solution.py:14
  159.2 0.0 all-gather.2.cloned.1.call-update
  159.2 102.2 %all-gather.2.cloned.1.call-done = f32[8192,384]{1,0:T(8,128)} async-done(((f32[512,384]{1,0:T(8,128)}), f32[8192,384]{1,0:T(8,128)}) %all-gather.2.cloned.1.call-update) | async-done | bytes 12582928 | tf_op jit(solution)/shard_map/all_gather | solution.py:28
  261.4 23.9 %fusion = (f32[256,384]{0,1:T(8,128)S(1)}, f32[256,384]{0,1:T(8,128)S(1)}, f32[256,384]{0,1:T(8,128)S(1)}) fusion(f32[8192,384]{1,0:T(8,128)} %all-gather.2.cloned.1.call-done, f32[256,8192]{1,0:T(8,128)} %param.5), kind=kOutput, calls=%fused_computation.2 | convolution fusion | flops 9663873024 | bytes 22151168 | tf_op jit(solution)/shard_map/dot_general | solution.py:26
  285.4 0.6 sqrt_bitcast_fusion
  286.0 0.9 copy.6
  286.9 0.6 reduce_max.9
  (1 shorter events, 0.0 us)
Async XLA Ops:
  7.2 0.9 copy-start
  7.2 152.0 %reduce-scatter.2.cloned.1.call-start = ((), (), s32[]{:S(2)}) async-start(), calls=%async_computation.1 | async-start | bytes 13369344 | tf_op jit(solution)/shard_map/reduce_scatter | solution.py:14
  21.7 239.7 %all-gather.2.cloned.1.call-start = ((), (), s32[]{:S(2)}) async-start(), calls=%async_computation.2 | async-start | bytes 13369344 | tf_op jit(solution)/shard_map/all_gather | solution.py:28
Sparse Core Ops, SparseCore 0:
  21.8 137.3 reduce-scatter.1
  161.5 99.8 all-gather.1
where the time goes:
time: 295 us; the launch traced here: 294 us
  waiting for transfers between devices  239 us (81%)
  matrix products  37.5 us (13%)
  between operations  14.1 us (5%)
    reduce_scatter x1, waiting for transfers between devices, shards(): lax.psum_scatter(lax.dot_general(modal_map, histories, (((0,), (0,)), (()...  137 us
    all_gather x1, waiting for transfers between devices, shards(): lax.all_gather(modal_rows, 'rows', axis=0, tiled=True)  102 us
    dot_general x1, matrix products, shards(): jnp.dot(recovery, lax.all_gather(modal_rows, 'rows', axis=0, tiled=True),...  23.9 us
    dot_general x1, matrix products, shards(): lax.dot_general(modal_map, histories, (((0,), (0,)), ((), ())), precision...  13.6 us
  transfers between devices with their start and end apart: 2, of which 2 were waited for; matrix products, arithmetic and copies ran while one was open for 0% of the time, Pallas kernels for 0%

commit v1 on v0

v1 whole, which is shorter than its diff:
```python
import jax
import jax.numpy as jnp
from jax import lax
from jax.sharding import PartitionSpec as P

CASES = 4
CORES = 2

epsilon = 1e-06


def dot(a, b, a_dim, b_dim):
    return lax.dot_general(
        a,
        b,
        (((a_dim,), (b_dim,)), ((), ())),
        precision=lax.Precision.HIGH,
        preferred_element_type=jnp.float32,
    )


def sizes_of(total, step=128):
    parts = [2, 4, 4, 4, 2]
    if total % (16 * step):
        return [total]
    return [part * (total // 16) for part in parts]


def shards_of(grp, rows):
    sides = 2 if grp == 2 and rows % 4 == 0 else 1
    planes = rows // (sides * CORES)

    def index(z, y, c):
        return (z * sides + y) * CORES + c

    everyone = [(z, y, c) for z in range(planes) for y in range(sides) for c in range(CORES)]
    other_core = [(index(z, y, c), index(z, y, 1 - c)) for z, y, c in everyone]
    other_side = [(index(z, y, c), index(z, 1 - y, c)) for z, y, c in everyone]
    half = planes // 2

    def hop(moves):
        return [(index(z, y, c), index(moves[z], y, c)) for z, y, c in everyone if z in moves]

    inward = [hop({k: k + 1, planes - 1 - k: planes - 2 - k}) for k in range(half - 1)]
    across = hop({half - 1: half, half: half - 1})
    outward = [hop({k + 1: k, planes - 2 - k: planes - 1 - k}) for k in reversed(range(half - 1))]

    def send(value, pairs):
        return lax.ppermute(value, "rows", pairs)

    def shards(histories, modal_map, recovery):
        time_cols = histories.shape[1]
        modes = modal_map.shape[1]
        per_core = modes // CORES
        per_lane = per_core // sides
        place = lax.axis_index("rows")
        core = place % CORES
        side = (place // CORES) % sides
        z = place // (CORES * sides)

        sizes = sizes_of(per_lane)
        offsets = [sum(sizes[:k]) for k in range(len(sizes))]

        def columns(array, at_core, at_side, start, size):
            return lax.dynamic_slice_in_dim(array, at_core * per_core + at_side * per_lane + start, size, 1)

        def of_chip(array, at_side, start, size):
            give = columns(array, 1 - core, at_side, start, size)
            keep = columns(array, core, at_side, start, size)
            return keep, give

        near = [histories]
        if sides == 2:
            near.append(send(histories, other_side))

        def map_piece(start, size):
            kept, given = [], []
            for k in range(sides):
                at_side = side if k == 0 else 1 - side
                keep, give = of_chip(modal_map, at_side, start, size)
                kept.append(keep)
                given.append(columns(modal_map, 1 - core, at_side, start, size))
            got = send(jnp.stack(given), other_core)
            return [jnp.concatenate([kept[k], got[k]]) for k in range(sides)]

        first = map_piece(0, sizes[0])
        rest = map_piece(sizes[0], per_lane - sizes[0]) if len(sizes) > 1 else None

        def map_chunk(i, k):
            if i == 0:
                return first[k]
            return rest[k][:, offsets[i] - sizes[0] : offsets[i] - sizes[0] + sizes[i]]

        far_maps = []
        for i in range(len(sizes)):
            with jax.named_scope(f"far_map_chunk{i}"):
                far_maps.append(send(map_chunk(i, 1), other_side) if sides == 2 else None)
        far = send(jnp.stack(near), other_core)
        histories_here = [jnp.concatenate([near[k], far[k]]) for k in range(sides)]

        steps = len(inward) + 1 + len(outward)
        last = [None]

        def ordered(value):
            if last[0] is None:
                return value
            value, last[0] = lax.optimization_barrier((value, last[0]))
            return value

        held, flying = {}, {}
        recoveries = None
        total = None

        def advance(i, step):
            nonlocal total, recoveries
            if step == 0:
                value = dot(map_chunk(i, 0), histories_here[0], 0, 0)
                if sides == 2:
                    value = value + dot(ordered(far_maps[i]), histories_here[1], 0, 0)
            elif step <= steps:
                got = ordered(flying.pop(i))
                depth = half - 2 - (step - 1 - len(inward) - 1)
                if step - 1 <= len(inward):
                    value = held[i] + got
                else:
                    value = jnp.where((z == depth) | (z == planes - 1 - depth), got, held[i])
            else:
                cut = slice(offsets[i], offsets[i] + sizes[i])
                part = dot(recoveries[0][:, cut], held[i], 1, 0)
                if sides == 2:
                    part = part + dot(recoveries[1][:, cut], ordered(flying.pop(i)), 1, 0)
                total = part if total is None else total + part
                last[0] = total
                return
            held[i] = value
            last[0] = value
            if step < steps:
                flying[i] = send(value, (inward + [across] + outward)[step])
            elif sides == 2:
                flying[i] = send(value, other_side)

        for turn in range(len(sizes) + steps + 1):
            if turn == 2:
                source = ordered(recovery)
                recoveries = []
                for k in range(sides):
                    keep, give = of_chip(source, side if k == 0 else 1 - side, 0, per_lane)
                    recoveries.append(jnp.concatenate([keep, send(columns(source, 1 - core, side if k == 0 else 1 - side, 0, per_lane), other_core)]))
            for step in reversed(range(steps + 2)):
                i = turn - step
                if 0 <= i < len(sizes):
                    with jax.named_scope(f"chunk{i}_step{step}"):
                        advance(i, step)

        mine = recovery.shape[0]
        responses = total[:mine] + send(total[mine:], other_core)
        by_case = responses.reshape(mine, CASES, time_cols // CASES)
        peak_response = jnp.max(jnp.abs(by_case), axis=2).T
        rms_response = jnp.sqrt(jnp.mean(by_case * by_case, axis=2) + epsilon).T
        return (responses, peak_response, rms_response)

    return shards


def solution(mesh):
    return jax.shard_map(
        shards_of(mesh.shape["grp"], mesh.shape["rows"]),
        mesh=mesh,
        in_specs=(P(("grp", "rows"), None), P(("grp", "rows"), None), P(("grp", "rows"), None)),
        out_specs=(P(("grp", "rows"), None), P(None, ("grp", "rows")), P(None, ("grp", "rows"))),
        check_vma=False,
    )
```

time: 295 us -> 183 us (0.62)
  waiting for transfers between devices: 239 us -> 86.5 us
  starting transfers between devices: 0.26 us -> 49.1 us
  matrix products: 37.5 us -> 24.6 us
  between operations: 14.1 us -> 1.38 us
  local copies, waits for them, and re-layouts: 1.79 us -> 10.8 us
  other arithmetic: 1.27 us -> 9.52 us
    reduce_scatter x1 -> x0, waiting for transfers between devices: 137 us -> none  [shards(): lax.psum_scatter(lax.dot_general(modal_map, histories, (((0,), (0,)), (()...]
    all_gather x1 -> x0, waiting for transfers between devices: 102 us -> none  [shards(): lax.all_gather(modal_rows, 'rows', axis=0, tiled=True)]
    ppermute x0 -> x32, waiting for transfers between devices: none -> 86.5 us  [send(): return lax.ppermute(value, 'rows', pairs)]
    ppermute x0 -> x32, starting transfers between devices: none -> 49.1 us  [send(): return lax.ppermute(value, 'rows', pairs)]
    dot_general x2 -> x20, matrix products: 37.5 us -> 24.6 us  [dot(): lax.dot_general(a, b, (((a_dim,), (b_dim,)), ((), ())), precision=lax.Pre...]
    dynamic_slice x0 -> x3, local copies, waits for them, and re-layouts: none -> 7.23 us  [columns(): lax.dynamic_slice_in_dim(array, at_core * per_core + at_side * per_lane +...]
    add x0 -> x10, other arithmetic: none -> 4.36 us  [advance(): value = held[i] + got]
  transfers between devices with their start and end apart: 2 -> 32, of which waited for: 2 -> 15; matrix products, arithmetic and copies ran while one was open for 0% -> 17% of each run, Pallas kernels for 0% -> 0%
where the time goes in v1:
time: 183 us; the launch traced here: 182 us
  waiting for transfers between devices  86.5 us (47%)
  starting transfers between devices  49.1 us (27%)
  matrix products  24.6 us (13%)
  local copies, waits for them, and re-layouts  10.8 us (6%)
  other arithmetic  9.52 us (5%)
    ppermute x32, waiting for transfers between devices, send(): return lax.ppermute(value, 'rows', pairs)  86.5 us
    ppermute x32, starting transfers between devices, send(): return lax.ppermute(value, 'rows', pairs)  49.1 us
    dot_general x20, matrix products, dot(): lax.dot_general(a, b, (((a_dim,), (b_dim,)), ((), ())), precision=lax.Pre...  24.6 us
    dynamic_slice x3, local copies, waits for them, and re-layouts, columns(): lax.dynamic_slice_in_dim(array, at_core * per_core + at_side * per_lane +...  7.23 us
    add x10, other arithmetic, advance(): value = held[i] + got  4.36 us
  transfers between devices with their start and end apart: 32, of which 15 were waited for; matrix products, arithmetic and copies ran while one was open for 17% of the time, Pallas kernels for 0%

profile of v1, /device:TPU:0, one launch (start us, length us, event | category | flops | bytes accessed | tf_op | source)
XLA Modules:
  0.0 182.0 jit_solution(12022165797985152792)
XLA Ops:
  0.7 3.2 %constant_dynamic-slice_fusion.7 = (f32[128,1792]{1,0:T(8,128)S(1)}, f32[128,1792]{1,0:T(8,128)}, f32[1,128,1792]{2,1,0:T(8,128)S(1)}, f32[1,128,1792]{2,1,0:T(8,128)S(1)}) fusion(f32[128,8192]{1,0:T(8,128)} %param.4, s32[]{:T(128)S(6)} %select_n.77, s32[]{:T(128)S(6)} %select_n.80, s32[]{:T(128)S(6)} %select_n.79, s32[]{:T(128)S(6)} %select_n.78), kind=kLoop, calls=%fused_computation.106 | loop fusion | bytes 7340048 | tf_op jit(solution)/shard_map/dynamic_slice | solution.py:65
  5.7 2.5 %collective-permute-start.1 = (f32[128,384]{1,0:T(8,128)S(1)}, f32[128,384]{1,0:T(8,128)S(1)}, u32[]{:S(2)}, u32[]{:S(2)}) collective-permute-start(f32[128,384]{1,0:T(8,128)S(1)} %copy-done.8), channel_id=1, source_target_pairs={{0,2},{1,3},{2,0},{3,1},{4,6},{5,7},{6,4},{7,5},{8,10},{9,11},{10,... | collective-permute-start | bytes 589832 | tf_op jit(solution)/shard_map/ppermute | solution.py:49
  9.7 4.1 %collective-permute-done.1 = f32[128,384]{1,0:T(8,128)S(1)} collective-permute-done((f32[128,384]{1,0:T(8,128)S(1)}, f32[128,384]{1,0:T(8,128)S(1)}, u32[]{:S(2)}, u32[]{:S(2)}) %collective-permute-start.1) | collective-permute-done | bytes 196640 | tf_op jit(solution)/shard_map/ppermute | solution.py:49
  15.8 6.9 %collective-permute-done.5 = f32[256,256]{1,0:T(8,128)S(1)} collective-permute-done((f32[256,256]{1,0:T(8,128)S(1)}, f32[256,256]{1,0:T(8,128)S(1)}, u32[]{:S(2)}, u32[]{:S(2)}) %collective-permute-start.5) | collective-permute-done | bytes 262176 | tf_op jit(solution)/shard_map/far_map_chunk0/ppermute | solution.py:49
  28.1 3.8 %collective-permute-start.6 = (f32[256,384]{1,0:T(8,128)S(1)}, f32[256,384]{1,0:T(8,128)S(1)}, u32[]{:S(2)}, u32[]{:S(2)}) collective-permute-start(f32[256,384]{1,0:T(8,128)S(1)} %convolution_add_fusion.9), channel_id=1, source_target_pairs={{0,4},{1,5},{2,6},{3,7},{12,8},{13,9},{14,10},{15,11},{16,20},{17,... | collective-permute-start | bytes 1179656 | tf_op jit(solution)/shard_map/chunk0_step0/ppermute | solution.py:49
  31.9 7.9 %collective-permute-done.6 = f32[256,384]{1,0:T(8,128)S(1)} collective-permute-done((f32[256,384]{1,0:T(8,128)S(1)}, f32[256,384]{1,0:T(8,128)S(1)}, u32[]{:S(2)}, u32[]{:S(2)}) %collective-permute-start.6) | collective-permute-done | bytes 393248 | tf_op jit(solution)/shard_map/chunk0_step0/ppermute | solution.py:49
  41.2 4.4 %collective-permute-start.11 = (f32[512,384]{1,0:T(8,128)S(1)}, f32[512,384]{1,0:T(8,128)S(1)}, u32[]{:S(2)}, u32[]{:S(2)}) collective-permute-start(f32[512,384]{1,0:T(8,128)S(1)} %convolution_add_fusion.7), channel_id=1, source_target_pairs={{0,4},{1,5},{2,6},{3,7},{12,8},{13,9},{14,10},{15,11},{16,20},{17,... | collective-permute-start | bytes 2359304 | tf_op jit(solution)/shard_map/chunk1_step0/ppermute | solution.py:49
  46.8 2.9 %constant_dynamic-slice_fusion.3 = (f32[256,2048]{1,0:T(8,128)S(1)}, f32[256,2048]{1,0:T(8,128)}, f32[256,2048]{1,0:T(8,128)}, f32[256,2048]{1,0:T(8,128)}) fusion(f32[256,8192]{1,0:T(8,128)S(1)} %bitcast.43, s32[]{:T(128)S(6)} %select_n.81, s32[]{:T(128)S(6)} %select_n.83, s32[]{:T(128)S(6)} %select_n.84, s32[]{:T(128)S(6)} %select_n.82), kind=kLoop, calls=%fused_computation.102 | loop fusion | bytes 16777232 | tf_op jit(solution)/shard_map/dynamic_slice | solution.py:65
  51.8 9.3 %collective-permute-done.11 = f32[512,384]{1,0:T(8,128)S(1)} collective-permute-done((f32[512,384]{1,0:T(8,128)S(1)}, f32[512,384]{1,0:T(8,128)S(1)}, u32[]{:S(2)}, u32[]{:S(2)}) %collective-permute-start.11) | collective-permute-done | bytes 786464 | tf_op jit(solution)/shard_map/chunk1_step0/ppermute | solution.py:49
  65.7 7.2 %collective-permute-start.15 = (f32[512,384]{1,0:T(8,128)}, f32[512,384]{1,0:T(8,128)}, u32[]{:S(2)}, u32[]{:S(2)}) collective-permute-start(f32[512,384]{1,0:T(8,128)} %convolution_add_fusion.6), channel_id=1, source_target_pairs={{0,4},{1,5},{2,6},{3,7},{12,8},{13,9},{14,10},{15,11},{16,20},{17,... | collective-permute-start | bytes 2359304 | tf_op jit(solution)/shard_map/chunk2_step0/ppermute | solution.py:49
  78.3 8.3 %collective-permute-done.15 = f32[512,384]{1,0:T(8,128)} collective-permute-done((f32[512,384]{1,0:T(8,128)}, f32[512,384]{1,0:T(8,128)}, u32[]{:S(2)}, u32[]{:S(2)}) %collective-permute-start.15) | collective-permute-done | bytes 786464 | tf_op jit(solution)/shard_map/chunk2_step0/ppermute | solution.py:49
  93.2 5.6 %collective-permute-start.20 = (f32[512,384]{1,0:T(8,128)S(1)}, f32[512,384]{1,0:T(8,128)S(1)}, u32[]{:S(2)}, u32[]{:S(2)}) collective-permute-start(f32[512,384]{1,0:T(8,128)S(1)} %convolution_add_fusion.4), channel_id=1, source_target_pairs={{0,4},{1,5},{2,6},{3,7},{12,8},{13,9},{14,10},{15,11},{16,20},{17,... | collective-permute-start | bytes 2359304 | tf_op jit(solution)/shard_map/chunk3_step0/ppermute | solution.py:49
  101.8 2.7 %collective-permute-done.17 = f32[512,384]{1,0:T(8,128)S(1)} collective-permute-done((f32[512,384]{1,0:T(8,128)S(1)}, f32[512,384]{1,0:T(8,128)S(1)}, u32[]{:S(2)}, u32[]{:S(2)}) %collective-permute-start.17) | collective-permute-done | bytes 786464 | tf_op jit(solution)/shard_map/chunk1_step2/ppermute | solution.py:49
  108.1 3.5 %collective-permute-done.20 = f32[512,384]{1,0:T(8,128)S(1)} collective-permute-done((f32[512,384]{1,0:T(8,128)S(1)}, f32[512,384]{1,0:T(8,128)S(1)}, u32[]{:S(2)}, u32[]{:S(2)}) %collective-permute-start.20) | collective-permute-done | bytes 786464 | tf_op jit(solution)/shard_map/chunk3_step0/ppermute | solution.py:49
  112.6 12.6 %collective-permute-done.19 = f32[256,256]{1,0:T(8,128)S(1)} collective-permute-done((f32[256,256]{1,0:T(8,128)S(1)}, f32[256,256]{1,0:T(8,128)S(1)}, u32[]{:S(2)}, u32[]{:S(2)}) %collective-permute-start.19) | collective-permute-done | bytes 262176 | tf_op jit(solution)/shard_map/far_map_chunk4/ppermute | solution.py:49
  126.1 1.9 %fusion.8 = f32[512,384]{0,1:T(8,128)S(1)} fusion(f32[512,384]{1,0:T(8,128)S(1)} %collective-permute-done.18, f32[256,2048]{1,0:T(8,128)S(1)} %copy-done, f32[256,2048]{1,0:T(8,128)} %collective-permute-done.12), kind=kOutput, calls=%fused_computation.42 | convolution fusion | flops 604241920 | bytes 5767168 | tf_op jit(solution)/shard_map/chunk1_step4/dot_general | solution.py:13
  128.0 1.9 %fusion.1 = f32[512,384]{0,1:T(8,128)S(1)} fusion(f32[512,384]{0,1:T(8,128)S(1)} %convolution_add_fusion.5, f32[512,384]{0,1:T(8,128)S(1)} %fusion.8, f32[512,384]{1,0:T(8,128)S(1)} %broadcast_select_fusion.2, f32[256,2048]{1,0:T(8,128)S(1)} %get-tuple-element.56, f32[256,2048]{1,0:T(8,128)} %collective-permute-done.7), kind=kOutput, calls=%fused_computation.34 | convolution fusion | flops 604635136 | bytes 7340032 | tf_op jit(solution)/shard_map/chunk1_step4/dot_general | solution.py:13
  134.6 3.9 %collective-permute-done.24 = f32[256,384]{1,0:T(8,128)S(1)} collective-permute-done((f32[256,384]{1,0:T(8,128)S(1)}, f32[256,384]{1,0:T(8,128)S(1)}, u32[]{:S(2)}, u32[]{:S(2)}) %collective-permute-start.24) | collective-permute-done | bytes 393248 | tf_op jit(solution)/shard_map/chunk4_step0/ppermute | solution.py:49
  138.5 5.9 %collective-permute-done.23 = f32[512,384]{1,0:T(8,128)S(1)} collective-permute-done((f32[512,384]{1,0:T(8,128)S(1)}, f32[512,384]{1,0:T(8,128)S(1)}, u32[]{:S(2)}, u32[]{:S(2)}) %collective-permute-start.23) | collective-permute-done | bytes 786464 | tf_op jit(solution)/shard_map/chunk2_step3/ppermute | solution.py:49
  146.3 1.9 %fusion.2 = f32[512,384]{0,1:T(8,128)S(1)} fusion(f32[512,384]{0,1:T(8,128)S(1)} %fusion.1, f32[512,384]{0,1:T(8,128)S(1)} %fusion.11, f32[512,384]{1,0:T(8,128)S(1)} %broadcast_select_fusion.1, f32[256,2048]{1,0:T(8,128)S(1)} %get-tuple-element.56, f32[256,2048]{1,0:T(8,128)} %collective-permute-done.7), kind=kOutput, calls=%fused_computation.35 | convolution fusion | flops 604635136 | bytes 7340032 | tf_op jit(solution)/shard_map/chunk2_step4/dot_general | solution.py:13
  152.1 11.0 %collective-permute-done.27 = f32[512,384]{1,0:T(8,128)S(1)} collective-permute-done((f32[512,384]{1,0:T(8,128)S(1)}, f32[512,384]{1,0:T(8,128)S(1)}, u32[]{:S(2)}, u32[]{:S(2)}) %collective-permute-start.27) | collective-permute-done | bytes 786464 | tf_op jit(solution)/shard_map/chunk3_step3/ppermute | solution.py:49
  163.1 1.9 %fusion.5 = f32[512,384]{0,1:T(8,128)S(1)} fusion(f32[512,384]{1,0:T(8,128)S(1)} %collective-permute-done.27, f32[256,2048]{1,0:T(8,128)S(1)} %copy-done, f32[256,2048]{1,0:T(8,128)} %collective-permute-done.12), kind=kOutput, calls=%fused_computation.40 | convolution fusion | flops 604241920 | bytes 5767168 | tf_op jit(solution)/shard_map/chunk3_step4/dot_general | solution.py:13
  165.0 1.9 %fusion.3 = f32[512,384]{0,1:T(8,128)S(1)} fusion(f32[512,384]{0,1:T(8,128)S(1)} %fusion.2, f32[512,384]{0,1:T(8,128)S(1)} %fusion.5, f32[512,384]{1,0:T(8,128)S(1)} %broadcast_select_fusion, f32[256,2048]{1,0:T(8,128)S(1)} %get-tuple-element.56, f32[256,2048]{1,0:T(8,128)} %collective-permute-done.7), kind=kOutput, calls=%fused_computation.36 | convolution fusion | flops 604635136 | bytes 7340032 | tf_op jit(solution)/shard_map/chunk3_step4/dot_general | solution.py:13
  167.8 7.0 %collective-permute-done.30 = f32[256,384]{1,0:T(8,128)S(1)} collective-permute-done((f32[256,384]{1,0:T(8,128)S(1)}, f32[256,384]{1,0:T(8,128)S(1)}, u32[]{:S(2)}, u32[]{:S(2)}) %collective-permute-start.30) | collective-permute-done | bytes 393248 | tf_op jit(solution)/shard_map/chunk4_step3/ppermute | solution.py:49
  (129 shorter events, 58.5 us)
Async XLA Ops:
  5.3 17.9 %collective-permute-start = (f32[2,128,1792]{2,1,0:T(8,128)}, f32[2,128,1792]{2,1,0:T(8,128)}, u32[]{:S(2)}, u32[]{:S(2)}) collective-permute-start(f32[2,128,1792]{2,1,0:T(8,128)} %pad_maximum_fusion), channel_id=1, source_target_pairs={{0,1},{1,0},{2,3},{3,2},{4,5},{5,4},{6,7},{7,6},{8,9},{9,8},{10,11... | collective-permute-start | bytes 5505032 | tf_op jit(solution)/shard_map/ppermute | solution.py:49
  14.0 8.8 %collective-permute-start.5 = (f32[256,256]{1,0:T(8,128)S(1)}, f32[256,256]{1,0:T(8,128)S(1)}, u32[]{:S(2)}, u32[]{:S(2)}) collective-permute-start(f32[256,256]{1,0:T(8,128)S(1)} %pad_maximum_fusion.12), channel_id=1, source_target_pairs={{0,2},{1,3},{2,0},{3,1},{4,6},{5,7},{6,4},{7,5},{8,10},{9,11},{10,... | collective-permute-start | bytes 786440 | tf_op jit(solution)/shard_map/far_map_chunk0/ppermute | solution.py:49
  26.0 13.9 %collective-permute-start.3 = (f32[256,512]{1,0:T(8,128)S(1)}, f32[256,512]{1,0:T(8,128)S(1)}, u32[]{:S(2)}, u32[]{:S(2)}) collective-permute-start(f32[256,512]{1,0:T(8,128)S(1)} %get-tuple-element.69), channel_id=1, source_target_pairs={{0,2},{1,3},{2,0},{3,1},{4,6},{5,7},{6,4},{7,5},{8,10},{9,11},{10,... | collective-permute-start | bytes 1572872 | tf_op jit(solution)/shard_map/far_map_chunk1/ppermute | solution.py:49
  28.1 11.7 %collective-permute-start.6 = (f32[256,384]{1,0:T(8,128)S(1)}, f32[256,384]{1,0:T(8,128)S(1)}, u32[]{:S(2)}, u32[]{:S(2)}) collective-permute-start(f32[256,384]{1,0:T(8,128)S(1)} %convolution_add_fusion.9), channel_id=1, source_target_pairs={{0,4},{1,5},{2,6},{3,7},{12,8},{13,9},{14,10},{15,11},{16,20},{17,... | collective-permute-start | bytes 1179656 | tf_op jit(solution)/shard_map/chunk0_step0/ppermute | solution.py:49
  41.2 19.8 %collective-permute-start.11 = (f32[512,384]{1,0:T(8,128)S(1)}, f32[512,384]{1,0:T(8,128)S(1)}, u32[]{:S(2)}, u32[]{:S(2)}) collective-permute-start(f32[512,384]{1,0:T(8,128)S(1)} %convolution_add_fusion.7), channel_id=1, source_target_pairs={{0,4},{1,5},{2,6},{3,7},{12,8},{13,9},{14,10},{15,11},{16,20},{17,... | collective-permute-start | bytes 2359304 | tf_op jit(solution)/shard_map/chunk1_step0/ppermute | solution.py:49
  46.3 17.2 %collective-permute-start.10 = (f32[256,512]{1,0:T(8,128)S(1)}, f32[256,512]{1,0:T(8,128)S(1)}, u32[]{:S(2)}, u32[]{:S(2)}) collective-permute-start(f32[256,512]{1,0:T(8,128)S(1)} %get-tuple-element.70), channel_id=1, source_target_pairs={{0,2},{1,3},{2,0},{3,1},{4,6},{5,7},{6,4},{7,5},{8,10},{9,11},{10,... | collective-permute-start | bytes 1572872 | tf_op jit(solution)/shard_map/far_map_chunk2/ppermute | solution.py:49
  49.7 49.0 %collective-permute-start.12 = (f32[256,2048]{1,0:T(8,128)}, f32[256,2048]{1,0:T(8,128)}, u32[]{:S(2)}, u32[]{:S(2)}) collective-permute-start(f32[256,2048]{1,0:T(8,128)} %get-tuple-element.57), channel_id=1, source_target_pairs={{0,1},{1,0},{2,3},{3,2},{4,5},{5,4},{6,7},{7,6},{8,9},{9,8},{10,11... | collective-permute-start | bytes 6291464 | tf_op jit(solution)/shard_map/ppermute | solution.py:49
  49.7 50.5 %collective-permute-start.7 = (f32[256,2048]{1,0:T(8,128)}, f32[256,2048]{1,0:T(8,128)}, u32[]{:S(2)}, u32[]{:S(2)}) collective-permute-start(f32[256,2048]{1,0:T(8,128)} %get-tuple-element.59), channel_id=1, source_target_pairs={{0,1},{1,0},{2,3},{3,2},{4,5},{5,4},{6,7},{7,6},{8,9},{9,8},{10,11... | collective-permute-start | bytes 6291464 | tf_op jit(solution)/shard_map/ppermute | solution.py:49
  50.3 22.6 %collective-permute-start.9 = (f32[256,384]{1,0:T(8,128)S(1)}, f32[256,384]{1,0:T(8,128)S(1)}, u32[]{:S(2)}, u32[]{:S(2)}) collective-permute-start(f32[256,384]{1,0:T(8,128)S(1)} %add.181), channel_id=1, source_target_pairs={{4,0},{5,1},{6,2},{7,3},{8,12},{9,13},{10,14},{11,15},{20,16},{21,... | collective-permute-start | bytes 1179656 | tf_op jit(solution)/shard_map/chunk0_step2/ppermute | solution.py:49
  62.0 13.5 %collective-permute-start.16 = (f32[512,384]{1,0:T(8,128)}, f32[512,384]{1,0:T(8,128)}, u32[]{:S(2)}, u32[]{:S(2)}) collective-permute-start(f32[512,384]{1,0:T(8,128)} %add.182), channel_id=1, source_target_pairs={{4,8},{5,9},{6,10},{7,11},{8,4},{9,5},{10,6},{11,7},{20,24},{21,25... | collective-permute-start | bytes 2359304 | tf_op jit(solution)/shard_map/chunk1_step1/ppermute | solution.py:49
  65.7 20.9 %collective-permute-start.15 = (f32[512,384]{1,0:T(8,128)}, f32[512,384]{1,0:T(8,128)}, u32[]{:S(2)}, u32[]{:S(2)}) collective-permute-start(f32[512,384]{1,0:T(8,128)} %convolution_add_fusion.6), channel_id=1, source_target_pairs={{0,4},{1,5},{2,6},{3,7},{12,8},{13,9},{14,10},{15,11},{16,20},{17,... | collective-permute-start | bytes 2359304 | tf_op jit(solution)/shard_map/chunk2_step0/ppermute | solution.py:49
  73.7 15.7 %collective-permute-start.14 = (f32[256,512]{1,0:T(8,128)}, f32[256,512]{1,0:T(8,128)}, u32[]{:S(2)}, u32[]{:S(2)}) collective-permute-start(f32[256,512]{1,0:T(8,128)} %get-tuple-element.68), channel_id=1, source_target_pairs={{0,2},{1,3},{2,0},{3,1},{4,6},{5,7},{6,4},{7,5},{8,10},{9,11},{10,... | collective-permute-start | bytes 1572872 | tf_op jit(solution)/shard_map/far_map_chunk3/ppermute | solution.py:49
  75.5 17.7 %collective-permute-start.13 = (f32[256,384]{1,0:T(8,128)S(1)}, f32[256,384]{1,0:T(8,128)S(1)}, u32[]{:S(2)}, u32[]{:S(2)}) collective-permute-start(f32[256,384]{1,0:T(8,128)S(1)} %broadcast_select_fusion.4), channel_id=1, source_target_pairs={{0,2},{1,3},{2,0},{3,1},{4,6},{5,7},{6,4},{7,5},{8,10},{9,11},{10,... | collective-permute-start | bytes 1179656 | tf_op jit(solution)/shard_map/chunk0_step3/ppermute | solution.py:49
  86.6 17.8 %collective-permute-start.17 = (f32[512,384]{1,0:T(8,128)S(1)}, f32[512,384]{1,0:T(8,128)S(1)}, u32[]{:S(2)}, u32[]{:S(2)}) collective-permute-start(f32[512,384]{1,0:T(8,128)S(1)} %add.184), channel_id=1, source_target_pairs={{4,0},{5,1},{6,2},{7,3},{8,12},{9,13},{10,14},{11,15},{20,16},{21,... | collective-permute-start | bytes 2359304 | tf_op jit(solution)/shard_map/chunk1_step2/ppermute | solution.py:49
  89.4 17.3 %collective-permute-start.21 = (f32[512,384]{1,0:T(8,128)S(1)}, f32[512,384]{1,0:T(8,128)S(1)}, u32[]{:S(2)}, u32[]{:S(2)}) collective-permute-start(f32[512,384]{1,0:T(8,128)S(1)} %add.185), channel_id=1, source_target_pairs={{4,8},{5,9},{6,10},{7,11},{8,4},{9,5},{10,6},{11,7},{20,24},{21,25... | collective-permute-start | bytes 2359304 | tf_op jit(solution)/shard_map/chunk2_step1/ppermute | solution.py:49
  93.2 18.4 %collective-permute-start.20 = (f32[512,384]{1,0:T(8,128)S(1)}, f32[512,384]{1,0:T(8,128)S(1)}, u32[]{:S(2)}, u32[]{:S(2)}) collective-permute-start(f32[512,384]{1,0:T(8,128)S(1)} %convolution_add_fusion.4), channel_id=1, source_target_pairs={{0,4},{1,5},{2,6},{3,7},{12,8},{13,9},{14,10},{15,11},{16,20},{17,... | collective-permute-start | bytes 2359304 | tf_op jit(solution)/shard_map/chunk3_step0/ppermute | solution.py:49
  104.5 21.6 %collective-permute-start.18 = (f32[512,384]{1,0:T(8,128)S(1)}, f32[512,384]{1,0:T(8,128)S(1)}, u32[]{:S(2)}, u32[]{:S(2)}) collective-permute-start(f32[512,384]{1,0:T(8,128)S(1)} %broadcast_select_fusion.2), channel_id=1, source_target_pairs={{0,2},{1,3},{2,0},{3,1},{4,6},{5,7},{6,4},{7,5},{8,10},{9,11},{10,... | collective-permute-start | bytes 2359304 | tf_op jit(solution)/shard_map/chunk1_step3/ppermute | solution.py:49
  106.0 19.2 %collective-permute-start.19 = (f32[256,256]{1,0:T(8,128)S(1)}, f32[256,256]{1,0:T(8,128)S(1)}, u32[]{:S(2)}, u32[]{:S(2)}) collective-permute-start(f32[256,256]{1,0:T(8,128)S(1)} %pad_maximum_fusion.8), channel_id=1, source_target_pairs={{0,2},{1,3},{2,0},{3,1},{4,6},{5,7},{6,4},{7,5},{8,10},{9,11},{10,... | collective-permute-start | bytes 786440 | tf_op jit(solution)/shard_map/far_map_chunk4/ppermute | solution.py:49
  106.8 23.1 %collective-permute-start.22 = (f32[512,384]{1,0:T(8,128)S(1)}, f32[512,384]{1,0:T(8,128)S(1)}, u32[]{:S(2)}, u32[]{:S(2)}) collective-permute-start(f32[512,384]{1,0:T(8,128)S(1)} %add.188), channel_id=1, source_target_pairs={{4,0},{5,1},{6,2},{7,3},{8,12},{9,13},{10,14},{11,15},{20,16},{21,... | collective-permute-start | bytes 2359304 | tf_op jit(solution)/shard_map/chunk2_step2/ppermute | solution.py:49
  111.7 21.5 %collective-permute-start.25 = (f32[512,384]{1,0:T(8,128)S(1)}, f32[512,384]{1,0:T(8,128)S(1)}, u32[]{:S(2)}, u32[]{:S(2)}) collective-permute-start(f32[512,384]{1,0:T(8,128)S(1)} %add.189), channel_id=1, source_target_pairs={{4,8},{5,9},{6,10},{7,11},{8,4},{9,5},{10,6},{11,7},{20,24},{21,25... | collective-permute-start | bytes 2359304 | tf_op jit(solution)/shard_map/chunk3_step1/ppermute | solution.py:49
  130.0 14.4 %collective-permute-start.23 = (f32[512,384]{1,0:T(8,128)S(1)}, f32[512,384]{1,0:T(8,128)S(1)}, u32[]{:S(2)}, u32[]{:S(2)}) collective-permute-start(f32[512,384]{1,0:T(8,128)S(1)} %broadcast_select_fusion.1), channel_id=1, source_target_pairs={{0,2},{1,3},{2,0},{3,1},{4,6},{5,7},{6,4},{7,5},{8,10},{9,11},{10,... | collective-permute-start | bytes 2359304 | tf_op jit(solution)/shard_map/chunk2_step3/ppermute | solution.py:49
  133.3 15.9 %collective-permute-start.26 = (f32[512,384]{1,0:T(8,128)S(1)}, f32[512,384]{1,0:T(8,128)S(1)}, u32[]{:S(2)}, u32[]{:S(2)}) collective-permute-start(f32[512,384]{1,0:T(8,128)S(1)} %add.193), channel_id=1, source_target_pairs={{4,0},{5,1},{6,2},{7,3},{8,12},{9,13},{10,14},{11,15},{20,16},{21,... | collective-permute-start | bytes 2359304 | tf_op jit(solution)/shard_map/chunk3_step2/ppermute | solution.py:49
  149.3 13.9 %collective-permute-start.27 = (f32[512,384]{1,0:T(8,128)S(1)}, f32[512,384]{1,0:T(8,128)S(1)}, u32[]{:S(2)}, u32[]{:S(2)}) collective-permute-start(f32[512,384]{1,0:T(8,128)S(1)} %broadcast_select_fusion), channel_id=1, source_target_pairs={{0,2},{1,3},{2,0},{3,1},{4,6},{5,7},{6,4},{7,5},{8,10},{9,11},{10,... | collective-permute-start | bytes 2359304 | tf_op jit(solution)/shard_map/chunk3_step3/ppermute | solution.py:49
  150.8 16.1 %collective-permute-start.29 = (f32[256,384]{1,0:T(8,128)S(1)}, f32[256,384]{1,0:T(8,128)S(1)}, u32[]{:S(2)}, u32[]{:S(2)}) collective-permute-start(f32[256,384]{1,0:T(8,128)S(1)} %add.197), channel_id=1, source_target_pairs={{4,0},{5,1},{6,2},{7,3},{8,12},{9,13},{10,14},{11,15},{20,16},{21,... | collective-permute-start | bytes 1179656 | tf_op jit(solution)/shard_map/chunk4_step2/ppermute | solution.py:49
  (25 other events, 270.4 us)

commit v2 on v0

v2 whole, which is shorter than its diff:
```python
import jax
import jax.numpy as jnp
from jax import lax
from jax.experimental import pallas as pl
from jax.experimental.pallas import tpu as pltpu
from jax.sharding import PartitionSpec as P

CASES = 4
CORES = 2
PARTS = [2, 2, 2, 2, 2, 2, 2, 2]
GROUPS = [[0], [1, 2], [3, 4, 5, 6, 7]]
JOINED = []
COSTS = [500000000, 500000000, 500000000, 1, 1, 500000000, 2000000000]
ORDER = "m0 m1 0.0 m2 rs 1.0 rw 0.1 1.1 2.0 0.2 2.1 1.2 0.3 3.0 4.0 2.2 1.3 0.4 3.1 5.0 2.3 1.4 4.1 3.2 6.0 2.4 5.1 4.2 3.3 6.1 7.0 5.2 4.3 3.4 6.2 7.1 5.3 4.4 6.3 7.2 5.4 6.4 7.3 7.4"

epsilon = 1e-06

VMEM = pl.BlockSpec(memory_space=pltpu.VMEM)
ANYWHERE = pl.BlockSpec(memory_space=pl.ANY)


PARAMS = pltpu.CompilerParams(vmem_limit_bytes=16 * 1024 * 1024)


def cost(kind):
    return pl.CostEstimate(flops=COSTS[kind], bytes_accessed=1, transcendentals=0)


def halves(value):
    high = value.astype(jnp.bfloat16)
    return high, (value - high.astype(jnp.float32)).astype(jnp.bfloat16)


def dot(a, b, a_dim):
    a_high, a_low = halves(a)
    b_high, b_low = halves(b)

    def product(x, y):
        return lax.dot_general(x, y, (((a_dim,), (0,)), ((), ())), preferred_element_type=jnp.float32)

    return product(a_high, b_high) + (product(a_high, b_low) + product(a_low, b_high))


def cut_kernel(cuts, at_ref, source, *refs):
    outs, sems = refs[: len(cuts)], refs[len(cuts)]
    copies = []
    for k, (which, begin, size) in enumerate(cuts):
        column = pl.multiple_of(at_ref[which] + begin, 128)
        copies.append(pltpu.make_async_copy(source.at[:, pl.ds(column, size)], outs[k], sems.at[k]))
        copies[-1].start()
    for copy in copies:
        copy.wait()


def cut(source, at, cuts, after=()):
    def kernel(at_ref, source_ref, *refs):
        cut_kernel(cuts, at_ref, source_ref, *refs[len(after) :])

    return pl.pallas_call(
        kernel,
        out_shape=[jax.ShapeDtypeStruct((source.shape[0], size), source.dtype) for _, _, size in cuts],
        in_specs=[pl.BlockSpec(memory_space=pltpu.SMEM), ANYWHERE] + [ANYWHERE] * len(after),
        out_specs=[ANYWHERE] * len(cuts),
        scratch_shapes=[pltpu.SemaphoreType.DMA((len(cuts),))],
        cost_estimate=cost(5),
        compiler_params=PARAMS,
        name="cut_columns",
    )(at, source, *after)


def join(parts, passed, after):
    rows = sum(part.shape[0] for part in parts)
    count = len(parts)

    def kernel(*refs):
        out = refs[count + len(passed) + len(after)]
        begin = 0
        for ref in refs[:count]:
            out[begin : begin + ref.shape[0]] = ref[...]
            begin += ref.shape[0]

    return pl.pallas_call(
        kernel,
        out_shape=[jax.ShapeDtypeStruct((rows, parts[0].shape[1]), jnp.float32)]
        + [jax.ShapeDtypeStruct(piece.shape, piece.dtype) for piece in passed],
        in_specs=[VMEM] * count + [ANYWHERE] * (len(passed) + len(after)),
        out_specs=[VMEM] + [ANYWHERE] * len(passed),
        input_output_aliases={count + k: 1 + k for k in range(len(passed))},
        cost_estimate=cost(6),
        compiler_params=PARAMS,
        name="join",
    )(*parts, *passed, *after)


def plane_sum(at, modal_map, maps, histories, begin, past, size, after):
    count = len(maps) + 1
    pairs = len(histories)
    depth, width = modal_map.shape[0], histories[0].shape[1]

    def kernel(at_ref, *refs):
        sources, history_refs = refs[:count], refs[count : count + pairs]
        out, block, sems = refs[-3:]
        copies = []
        for k in range(count):
            if k == 0:
                source = sources[0].at[:, pl.ds(pl.multiple_of(at_ref[0] + begin, 128), size)]
            else:
                source = sources[k].at[:, pl.ds(past[k - 1], size)]
            copies.append(pltpu.make_async_copy(source, block.at[pl.ds(k * depth, depth)], sems.at[k]))
            copies[-1].start()
        past_block = jnp.concatenate([ref[...] for ref in history_refs])
        for copy in copies:
            copy.wait()
        out[...] = dot(block[...], past_block, 0)

    return pl.pallas_call(
        kernel,
        out_shape=jax.ShapeDtypeStruct((size, width), jnp.float32),
        in_specs=[pl.BlockSpec(memory_space=pltpu.SMEM), ANYWHERE]
        + [ANYWHERE] * len(maps)
        + [VMEM] * pairs
        + [ANYWHERE] * len(after),
        out_specs=VMEM,
        scratch_shapes=[
            pltpu.VMEM((count * depth, size), jnp.float32),
            pltpu.SemaphoreType.DMA((count,)),
        ],
        cost_estimate=cost(0),
        compiler_params=PARAMS,
        name="plane_sum",
    )(at, modal_map, *maps, *histories, *after)


def add(held, got, after):
    def kernel(held_ref, got_ref, *refs):
        refs[-1][...] = held_ref[...] + got_ref[...]

    return pl.pallas_call(
        kernel,
        out_shape=jax.ShapeDtypeStruct(held.shape, held.dtype),
        in_specs=[VMEM, VMEM] + [ANYWHERE] * len(after),
        out_specs=VMEM,
        cost_estimate=cost(1),
        compiler_params=PARAMS,
        name="add",
    )(held, got, *after)


def choose(takes, held, got, before, after):
    above = before.shape[0] if before is not None else 0

    def kernel(takes_ref, held_ref, got_ref, *refs):
        out = refs[-1]
        if above:
            out[:above] = refs[0][...]

        @pl.when(takes_ref[0] == 1)
        def _():
            out[above:] = got_ref[...]

        @pl.when(takes_ref[0] == 0)
        def _():
            out[above:] = held_ref[...]

    return pl.pallas_call(
        kernel,
        out_shape=jax.ShapeDtypeStruct((above + held.shape[0], held.shape[1]), held.dtype),
        in_specs=[pl.BlockSpec(memory_space=pltpu.SMEM), VMEM, VMEM]
        + [VMEM] * (above > 0)
        + [ANYWHERE] * len(after),
        out_specs=VMEM,
        cost_estimate=cost(3),
        compiler_params=PARAMS,
        name="choose",
    )(takes, held, got, *([before] if above else []), *after)


def recover(at, recovery, recovery_got, begin, parts, total, after):
    size = parts[0].shape[0]
    count = len(parts)
    mine = recovery.shape[0]
    has_total = total is not None
    sources = count * 2

    def kernel(at_ref, recovery_ref, got_ref, *refs):
        parts_refs = refs[:count]
        total_ref = refs[count] if has_total else None
        out, block, sems = refs[-3:]
        copies = []
        for k in range(count):
            for j, source in enumerate((recovery_ref, got_ref)):
                column = pl.multiple_of(at_ref[j * count + k] + begin, 128)
                copies.append(
                    pltpu.make_async_copy(
                        source.at[:, pl.ds(column, size)],
                        block.at[pl.ds(j * mine, mine), pl.ds(k * size, size)],
                        sems.at[2 * k + j],
                    )
                )
                copies[-1].start()
        part = jnp.concatenate([ref[...] for ref in parts_refs])
        for copy in copies:
            copy.wait()
        value = dot(block[...], part, 1)
        out[...] = value + total_ref[...] if has_total else value

    rows, columns = 2 * mine, parts[0].shape[1]
    return pl.pallas_call(
        kernel,
        out_shape=jax.ShapeDtypeStruct((rows, columns), jnp.float32),
        in_specs=[pl.BlockSpec(memory_space=pltpu.SMEM), ANYWHERE, ANYWHERE]
        + [VMEM] * count
        + [VMEM] * has_total
        + [ANYWHERE] * len(after),
        out_specs=VMEM,
        scratch_shapes=[pltpu.VMEM((rows, count * size), jnp.float32), pltpu.SemaphoreType.DMA((sources,))],
        cost_estimate=cost(4),
        compiler_params=PARAMS,
        name="recover",
    )(at, recovery, recovery_got, *parts, *([total] if has_total else []), *after)


def finish(responses):
    by_case = responses.reshape(responses.shape[0], CASES, responses.shape[1] // CASES)
    peak_response = jnp.max(jnp.abs(by_case), axis=2).T
    rms_response = jnp.sqrt(jnp.mean(by_case * by_case, axis=2) + epsilon).T
    return (responses, peak_response, rms_response)


def plain(histories, modal_map, recovery):
    modal_rows = lax.psum_scatter(
        lax.dot_general(
            modal_map,
            histories,
            (((0,), (0,)), ((), ())),
            precision=lax.Precision.HIGHEST,
            preferred_element_type=jnp.float32,
        ),
        "rows",
        scatter_dimension=0,
        tiled=True,
    )
    responses = jnp.dot(
        recovery,
        lax.all_gather(modal_rows, "rows", axis=0, tiled=True),
        precision=lax.Precision.HIGHEST,
        preferred_element_type=jnp.float32,
    )
    return finish(responses)


PLANES, SIDES = 4, 2


def index(z, y, c):
    return (z * SIDES + y) * CORES + c


def pairs_of(move):
    everyone = [(z, y, c) for z in range(PLANES) for y in range(SIDES) for c in range(CORES)]
    return [(index(*place), index(*move(*place))) for place in everyone if move(*place) is not None]


OTHER_CORE = pairs_of(lambda z, y, c: (z, y, 1 - c))
OTHER_SIDE = pairs_of(lambda z, y, c: (z, 1 - y, c))
OTHER_BOTH = pairs_of(lambda z, y, c: (z, 1 - y, 1 - c))
HOPS = [
    pairs_of(lambda z, y, c: (z ^ 1, y, c) if z in (0, 3) else None),
    pairs_of(lambda z, y, c: (3 - z, y, c) if z in (1, 2) else None),
    pairs_of(lambda z, y, c: (z ^ 1, y, c) if z in (1, 2) else None),
    OTHER_SIDE,
]


def send(value, pairs):
    return lax.ppermute(value, "rows", pairs)


def shards(histories, modal_map, recovery):
    modes = modal_map.shape[1]
    per_core = modes // CORES
    per_lane = per_core // SIDES
    place = lax.axis_index("rows")
    core, side, z = place % CORES, (place // CORES) % SIDES, place // (CORES * SIDES)
    outer = ((z == 0) | (z == PLANES - 1)).astype(jnp.int32).reshape(1)

    sizes = [part * (per_lane // 16) for part in PARTS]
    offsets = [sum(sizes[:k]) for k in range(len(sizes))]
    spans = [(offsets[group[0]], sum(sizes[i] for i in group)) for group in GROUPS]
    group_of = {i: g for g, group in enumerate(GROUPS) for i in group}

    lanes = [(core, side), (core, 1 - side), (1 - core, side), (1 - core, 1 - side)]
    at = jnp.stack([c * per_core + s * per_lane for c, s in lanes]).astype(jnp.int32)
    own = [core * per_core + side * per_lane, core * per_core + (1 - side) * per_lane]
    their = [side * per_lane, (1 - side) * per_lane]
    recovery_at = jnp.stack(own + their).astype(jnp.int32)
    other_half = ((1 - core) * per_core).astype(jnp.int32).reshape(1)

    cuts = [(2, 0, per_lane)] + [(k, *span) for span in spans for k in (1, 3)]
    pieces = list(cut(modal_map, at, cuts))
    map_from_core = send(pieces[0], OTHER_CORE)
    side_histories = send(histories, OTHER_SIDE)
    pieces = [pieces[1 + 2 * g : 3 + 2 * g] for g in range(len(GROUPS))]
    maps, held, flying = {}, {}, {}
    total, after, recovery_got, plane_histories = None, [], None, None
    for work in ORDER.split():
        if work[0] == "m":
            g = int(work[1:])
            if g == 1:
                joined = list(join([histories, side_histories], pieces[g], [map_from_core] + maps[0]))
                pieces[g] = joined[1:]
                plane_histories = [joined[0], send(joined[0], OTHER_CORE)]
                after = joined[:1]
            maps[g] = [send(piece, pairs) for piece, pairs in zip(pieces[g], [OTHER_SIDE, OTHER_BOTH])]
            continue
        if work == "rs":
            after = list(cut(recovery, other_half, [(0, 0, per_core)], after))
            recovery_got = send(after[0], OTHER_CORE)
            continue
        if work == "rw":
            after = after + [recovery_got]
            continue
        i, step = (int(part) for part in work.split("."))
        if step == 0:
            side_map, both_map = maps[group_of[i]]
            begin = offsets[i] - spans[group_of[i]][0]
            value = plane_sum(
                at, modal_map, [side_map, map_from_core, both_map], plane_histories,
                offsets[i], [begin, offsets[i], begin], sizes[i], after,
            )
        elif step <= 2:
            value = add(held[i], flying[i], after)
        elif step == 3:
            value = choose(outer, held[i], flying[i], held[i - 1] if i - 1 in JOINED else None, after)
        elif i in JOINED:
            continue
        else:
            first = i - 1 if i - 1 in JOINED else i
            parts = [held[i], flying[i]]
            value = total = recover(recovery_at, recovery, recovery_got, offsets[first], parts, total, after)
        after = [value]
        if step < 4:
            held[i] = value
            if step < 3 or i not in JOINED:
                flying[i] = send(value, HOPS[step])

    rows = recovery.shape[0]
    return finish(total[:rows] + send(total[rows:], OTHER_CORE))


def solution(mesh):
    return jax.shard_map(
        shards if (mesh.shape["grp"], mesh.shape["rows"]) == (2, 16) else plain,
        mesh=mesh,
        in_specs=(P(("grp", "rows"), None), P(("grp", "rows"), None), P(("grp", "rows"), None)),
        out_specs=(P(("grp", "rows"), None), P(None, ("grp", "rows")), P(None, ("grp", "rows"))),
        check_vma=False,
    )
```

time: 295 us -> 169 us (0.57)
  waiting for transfers between devices: 239 us -> 59.7 us
  starting transfers between devices: 0.26 us -> 69.5 us
  matrix products: 37.5 us -> 0 us
  Pallas kernels: 0 us -> 32.8 us
  between operations: 14.1 us -> 1.49 us
    reduce_scatter x1 -> x0, waiting for transfers between devices: 137 us -> none  [shards(): lax.psum_scatter(lax.dot_general(modal_map, histories, (((0,), (0,)), (()...]
    all_gather x1 -> x0, waiting for transfers between devices: 102 us -> none  [shards(): lax.all_gather(modal_rows, 'rows', axis=0, tiled=True)]
    ppermute x0 -> x43, starting transfers between devices: none -> 69.5 us  [send(): return lax.ppermute(value, 'rows', pairs)]
    ppermute x0 -> x43, waiting for transfers between devices: none -> 59.7 us  [send(): return lax.ppermute(value, 'rows', pairs)]
    dot_general x2 -> x0, matrix products: 37.5 us -> none  [the longest x1 23.9 us: shards(): jnp.dot(recovery, lax.all_gather(modal_rows, 'rows', axis=0, tiled=True),...]
    pallas_call x0 -> x43, Pallas kernels: none -> 32.8 us  [the longest x8 13.9 us: recover(): pl.pallas_call(kernel, out_shape=jax.ShapeDtypeStruct((rows, columns), jn...]
  transfers between devices with their start and end apart: 2 -> 43, of which waited for: 2 -> 16; matrix products, arithmetic and copies ran while one was open for 0% -> 0% of each run, Pallas kernels for 0% -> 16%
where the time goes in v2:
time: 169 us; the launch traced here: 168 us
  starting transfers between devices  69.5 us (41%)
  waiting for transfers between devices  59.7 us (35%)
  Pallas kernels  32.8 us (19%)
  local copies, waits for them, and re-layouts  3.51 us (2%)
    ppermute x43, starting transfers between devices, send(): return lax.ppermute(value, 'rows', pairs)  69.5 us
    ppermute x43, waiting for transfers between devices, send(): return lax.ppermute(value, 'rows', pairs)  59.7 us
    pallas_call x8, Pallas kernels, recover(): pl.pallas_call(kernel, out_shape=jax.ShapeDtypeStruct((rows, columns), jn...  13.9 us
    pallas_call x8, Pallas kernels, plane_sum(): pl.pallas_call(kernel, out_shape=jax.ShapeDtypeStruct((size, width), jnp....  11.7 us
    pallas_call x16, Pallas kernels, add(): pl.pallas_call(kernel, out_shape=jax.ShapeDtypeStruct(held.shape, held.dt...  3.66 us
  transfers between devices with their start and end apart: 43, of which 16 were waited for; matrix products, arithmetic and copies ran while one was open for 0% of the time, Pallas kernels for 16%

profile of v2, /device:TPU:0, one launch (start us, length us, event | category | flops | bytes accessed | tf_op | source)
XLA Modules:
  0.0 168.5 jit_solution(2293891286784904941)
XLA Ops:
  0.8 2.2 %copy-done.2 = f32[128,8192]{1,0:T(8,128)S(1)} copy-done((f32[128,8192]{1,0:T(8,128)S(1)}, f32[128,8192]{1,0:T(8,128)}, u32[]{:S(2)}) %copy-start.2) | copy-done | bytes 4194328
  2.9 1.9 %cut_columns.2 = (f32[128,2048]{1,0:T(8,128)S(1)}, f32[128,256]{1,0:T(8,128)S(1)}, f32[128,256]{1,0:T(8,128)S(1)}, f32[128,512]{1,0:T(8,128)S(1)}, f32[128,512]{...) custom-call(s32[4]{0:T(128)S(1)} %pad_add_fusion.2.at_ref, f32[128,8192]{1,0:T(8,128)S(1)} %copy-done.2), custom_call_target="tpu_custom_call" | custom-call | flops 500000000 | bytes 1 | tf_op jit(solution)/shard_map/cut_columns/pallas_call | solution.py:59
  5.4 2.6 %collective-permute-start.3 = (f32[128,384]{1,0:T(8,128)}, f32[128,384]{1,0:T(8,128)S(1)}, u32[]{:S(2)}, u32[]{:S(2)}) collective-permute-start(f32[128,384]{1,0:T(8,128)} %refs_0_.9), channel_id=1, source_target_pairs={{0,2},{1,3},{2,0},{3,1},{4,6},{5,7},{6,4},{7,5},{8,10},{9,11},{10,... | collective-permute-start | bytes 589832 | tf_op jit(solution)/shard_map/ppermute | solution.py:276
  9.5 7.3 %collective-permute-done.refs_5_.refs_1_ = f32[128,256]{1,0:T(8,128)S(1)} collective-permute-done((f32[128,256]{1,0:T(8,128)S(1)}, f32[128,256]{1,0:T(8,128)S(1)}, u32[]{:S(2)}, u32[]{:S(2)}) %collective-permute-start) | collective-permute-done | bytes 131104 | tf_op jit(solution)/shard_map/ppermute | solution.py:276
  16.7 2.3 %collective-permute-done.2.refs_6_.refs_3_ = f32[128,256]{1,0:T(8,128)S(1)} collective-permute-done((f32[128,256]{1,0:T(8,128)S(1)}, f32[128,256]{1,0:T(8,128)S(1)}, u32[]{:S(2)}, u32[]{:S(2)}) %collective-permute-start.2) | collective-permute-done | bytes 131104 | tf_op jit(solution)/shard_map/ppermute | solution.py:276
  25.8 3.5 %collective-permute-start.8 = (f32[256,384]{1,0:T(8,128)S(1)}, f32[256,384]{1,0:T(8,128)S(1)}, u32[]{:S(2)}, u32[]{:S(2)}) collective-permute-start(f32[256,384]{1,0:T(8,128)S(1)} %plane_sum.8.refs_0_.held_ref), channel_id=1, source_target_pairs={{0,4},{1,5},{2,6},{3,7},{12,8},{13,9},{14,10},{15,11},{16,20},{17,... | collective-permute-start | bytes 1179656 | tf_op jit(solution)/shard_map/ppermute | solution.py:276
  29.4 3.9 %collective-permute-done.9.refs_1_ = f32[128,512]{1,0:T(8,128)S(1)} collective-permute-done((f32[128,512]{1,0:T(8,128)S(1)}, f32[128,512]{1,0:T(8,128)S(1)}, u32[]{:S(2)}, u32[]{:S(2)}) %collective-permute-start.9) | collective-permute-done | bytes 262176 | tf_op jit(solution)/shard_map/ppermute | solution.py:276
  33.2 4.5 %collective-permute-done.10.refs_3_ = f32[128,512]{1,0:T(8,128)S(1)} collective-permute-done((f32[128,512]{1,0:T(8,128)S(1)}, f32[128,512]{1,0:T(8,128)S(1)}, u32[]{:S(2)}, u32[]{:S(2)}) %collective-permute-start.10) | collective-permute-done | bytes 262176 | tf_op jit(solution)/shard_map/ppermute | solution.py:276
  39.1 3.4 %collective-permute-start.12 = (f32[256,384]{1,0:T(8,128)S(1)}, f32[256,384]{1,0:T(8,128)S(1)}, u32[]{:S(2)}, u32[]{:S(2)}) collective-permute-start(f32[256,384]{1,0:T(8,128)S(1)} %plane_sum.9.refs_0_.held_ref), channel_id=1, source_target_pairs={{0,4},{1,5},{2,6},{3,7},{12,8},{13,9},{14,10},{15,11},{16,20},{17,... | collective-permute-start | bytes 1179656 | tf_op jit(solution)/shard_map/ppermute | solution.py:276
  45.2 6.6 %collective-permute-done.12.got_ref = f32[256,384]{1,0:T(8,128)S(1)} collective-permute-done((f32[256,384]{1,0:T(8,128)S(1)}, f32[256,384]{1,0:T(8,128)S(1)}, u32[]{:S(2)}, u32[]{:S(2)}) %collective-permute-start.12) | collective-permute-done | bytes 393248 | tf_op jit(solution)/shard_map/ppermute | solution.py:276
  52.6 2.1 %plane_sum.10.refs_0_.held_ref = f32[256,384]{1,0:T(8,128)} custom-call(s32[4]{0:T(128)S(1)} %pad_add_fusion.2.at_ref, f32[128,8192]{1,0:T(8,128)S(1)} %copy-done.3, f32[128,512]{1,0:T(8,128)S(1)} %collective-permute-done.9.refs_1_, f32[128,2048]{1,0:T(8,128)S(1)} %collective-permute-done.1.refs_4_.refs_2_, f32[128,512]{1,0:T(8,128)S(1)} %collective-permute-done.10.refs_3_, ...), custom_call_target="tpu_custom_call" | custom-call | flops 500000000 | bytes 1 | tf_op jit(solution)/shard_map/plane_sum/pallas_call | solution.py:116
  54.7 5.1 %collective-permute-start.15 = (f32[256,384]{1,0:T(8,128)}, f32[256,384]{1,0:T(8,128)}, u32[]{:S(2)}, u32[]{:S(2)}) collective-permute-start(f32[256,384]{1,0:T(8,128)} %plane_sum.10.refs_0_.held_ref), channel_id=1, source_target_pairs={{0,4},{1,5},{2,6},{3,7},{12,8},{13,9},{14,10},{15,11},{16,20},{17,... | collective-permute-start | bytes 1179656 | tf_op jit(solution)/shard_map/ppermute | solution.py:276
  62.6 5.3 %collective-permute-done.15.got_ref = f32[256,384]{1,0:T(8,128)} collective-permute-done((f32[256,384]{1,0:T(8,128)}, f32[256,384]{1,0:T(8,128)}, u32[]{:S(2)}, u32[]{:S(2)}) %collective-permute-start.15) | collective-permute-done | bytes 393248 | tf_op jit(solution)/shard_map/ppermute | solution.py:276
  78.0 5.5 %collective-permute-start.16 = (f32[256,384]{1,0:T(8,128)S(1)}, f32[256,384]{1,0:T(8,128)S(1)}, u32[]{:S(2)}, u32[]{:S(2)}) collective-permute-start(f32[256,384]{1,0:T(8,128)S(1)} %plane_sum.11.refs_6_.held_ref), channel_id=1, source_target_pairs={{0,4},{1,5},{2,6},{3,7},{12,8},{13,9},{14,10},{15,11},{16,20},{17,... | collective-permute-start | bytes 1179656 | tf_op jit(solution)/shard_map/ppermute | solution.py:276
  90.3 2.7 %collective-permute-done.16.got_ref = f32[256,384]{1,0:T(8,128)S(1)} collective-permute-done((f32[256,384]{1,0:T(8,128)S(1)}, f32[256,384]{1,0:T(8,128)S(1)}, u32[]{:S(2)}, u32[]{:S(2)}) %collective-permute-start.16) | collective-permute-done | bytes 393248 | tf_op jit(solution)/shard_map/ppermute | solution.py:276
  95.0 6.1 %collective-permute-start.27 = (f32[256,384]{1,0:T(8,128)S(1)}, f32[256,384]{1,0:T(8,128)S(1)}, u32[]{:S(2)}, u32[]{:S(2)}) collective-permute-start(f32[256,384]{1,0:T(8,128)S(1)} %plane_sum.13.refs_0_.held_ref), channel_id=1, source_target_pairs={{0,4},{1,5},{2,6},{3,7},{12,8},{13,9},{14,10},{15,11},{16,20},{17,... | collective-permute-start | bytes 1179656 | tf_op jit(solution)/shard_map/ppermute | solution.py:276
  107.0 4.6 %collective-permute-start.24 = (f32[256,384]{1,0:T(8,128)S(1)}, f32[256,384]{1,0:T(8,128)S(1)}, u32[]{:S(2)}, u32[]{:S(2)}) collective-permute-start(f32[256,384]{1,0:T(8,128)S(1)} %plane_sum.14.refs_3_.held_ref), channel_id=1, source_target_pairs={{0,4},{1,5},{2,6},{3,7},{12,8},{13,9},{14,10},{15,11},{16,20},{17,... | collective-permute-start | bytes 1179656 | tf_op jit(solution)/shard_map/ppermute | solution.py:276
  119.3 7.4 %collective-permute-start.29 = (f32[256,384]{1,0:T(8,128)S(1)}, f32[256,384]{1,0:T(8,128)S(1)}, u32[]{:S(2)}, u32[]{:S(2)}) collective-permute-start(f32[256,384]{1,0:T(8,128)S(1)} %plane_sum.15.refs_0_.held_ref), channel_id=1, source_target_pairs={{0,4},{1,5},{2,6},{3,7},{12,8},{13,9},{14,10},{15,11},{16,20},{17,... | collective-permute-start | bytes 1179656 | tf_op jit(solution)/shard_map/ppermute | solution.py:276
  133.0 4.8 %collective-permute-done.37.got_ref = f32[256,384]{1,0:T(8,128)S(1)} collective-permute-done((f32[256,384]{1,0:T(8,128)S(1)}, f32[256,384]{1,0:T(8,128)S(1)}, u32[]{:S(2)}, u32[]{:S(2)}) %collective-permute-start.37) | collective-permute-done | bytes 393248 | tf_op jit(solution)/shard_map/ppermute | solution.py:276
  138.2 2.0 %collective-permute-done.36.refs_1_ = f32[256,384]{1,0:T(8,128)S(1)} collective-permute-done((f32[256,384]{1,0:T(8,128)S(1)}, f32[256,384]{1,0:T(8,128)S(1)}, u32[]{:S(2)}, u32[]{:S(2)}) %collective-permute-start.36) | collective-permute-done | bytes 393248 | tf_op jit(solution)/shard_map/ppermute | solution.py:276
  141.9 2.4 %collective-permute-done.35.got_ref = f32[256,384]{1,0:T(8,128)S(1)} collective-permute-done((f32[256,384]{1,0:T(8,128)S(1)}, f32[256,384]{1,0:T(8,128)S(1)}, u32[]{:S(2)}, u32[]{:S(2)}) %collective-permute-start.35) | collective-permute-done | bytes 393248 | tf_op jit(solution)/shard_map/ppermute | solution.py:276
  145.8 1.9 %collective-permute-done.40.refs_1_ = f32[256,384]{1,0:T(8,128)S(1)} collective-permute-done((f32[256,384]{1,0:T(8,128)S(1)}, f32[256,384]{1,0:T(8,128)S(1)}, u32[]{:S(2)}, u32[]{:S(2)}) %collective-permute-start.40) | collective-permute-done | bytes 393248 | tf_op jit(solution)/shard_map/ppermute | solution.py:276
  149.4 4.2 %collective-permute-done.39.refs_1_ = f32[256,384]{1,0:T(8,128)S(1)} collective-permute-done((f32[256,384]{1,0:T(8,128)S(1)}, f32[256,384]{1,0:T(8,128)S(1)}, u32[]{:S(2)}, u32[]{:S(2)}) %collective-permute-start.39) | collective-permute-done | bytes 393248 | tf_op jit(solution)/shard_map/ppermute | solution.py:276
  156.2 7.0 %collective-permute-done.41.refs_1_ = f32[256,384]{1,0:T(8,128)S(1)} collective-permute-done((f32[256,384]{1,0:T(8,128)S(1)}, f32[256,384]{1,0:T(8,128)S(1)}, u32[]{:S(2)}, u32[]{:S(2)}) %collective-permute-start.41) | collective-permute-done | bytes 393248 | tf_op jit(solution)/shard_map/ppermute | solution.py:276
  (139 shorter events, 68.1 us)
Async XLA Ops:
  4.8 14.2 %collective-permute-start.1 = (f32[128,2048]{1,0:T(8,128)S(1)}, f32[128,2048]{1,0:T(8,128)S(1)}, u32[]{:S(2)}, u32[]{:S(2)}) collective-permute-start(f32[128,2048]{1,0:T(8,128)S(1)} %get-tuple-element.14), channel_id=1, source_target_pairs={{0,1},{1,0},{2,3},{3,2},{4,5},{5,4},{6,7},{7,6},{8,9},{9,8},{10,11... | collective-permute-start | bytes 3145736 | tf_op jit(solution)/shard_map/ppermute | solution.py:276
  5.4 13.7 %collective-permute-start.3 = (f32[128,384]{1,0:T(8,128)}, f32[128,384]{1,0:T(8,128)S(1)}, u32[]{:S(2)}, u32[]{:S(2)}) collective-permute-start(f32[128,384]{1,0:T(8,128)} %refs_0_.9), channel_id=1, source_target_pairs={{0,2},{1,3},{2,0},{3,1},{4,6},{5,7},{6,4},{7,5},{8,10},{9,11},{10,... | collective-permute-start | bytes 589832 | tf_op jit(solution)/shard_map/ppermute | solution.py:276
  23.9 18.6 %collective-permute-start.5 = (f32[256,4096]{1,0:T(8,128)S(1)}, f32[256,4096]{1,0:T(8,128)S(1)}, u32[]{:S(2)}, u32[]{:S(2)}) collective-permute-start(f32[256,4096]{1,0:T(8,128)S(1)} %cut_columns.3.refs_6_), channel_id=1, source_target_pairs={{0,1},{1,0},{2,3},{3,2},{4,5},{5,4},{6,7},{7,6},{8,9},{9,8},{10,11... | collective-permute-start | bytes 12582920 | tf_op jit(solution)/shard_map/ppermute | solution.py:276
  25.8 16.7 %collective-permute-start.8 = (f32[256,384]{1,0:T(8,128)S(1)}, f32[256,384]{1,0:T(8,128)S(1)}, u32[]{:S(2)}, u32[]{:S(2)}) collective-permute-start(f32[256,384]{1,0:T(8,128)S(1)} %plane_sum.8.refs_0_.held_ref), channel_id=1, source_target_pairs={{0,4},{1,5},{2,6},{3,7},{12,8},{13,9},{14,10},{15,11},{16,20},{17,... | collective-permute-start | bytes 1179656 | tf_op jit(solution)/shard_map/ppermute | solution.py:276
  39.1 12.7 %collective-permute-start.12 = (f32[256,384]{1,0:T(8,128)S(1)}, f32[256,384]{1,0:T(8,128)S(1)}, u32[]{:S(2)}, u32[]{:S(2)}) collective-permute-start(f32[256,384]{1,0:T(8,128)S(1)} %plane_sum.9.refs_0_.held_ref), channel_id=1, source_target_pairs={{0,4},{1,5},{2,6},{3,7},{12,8},{13,9},{14,10},{15,11},{16,20},{17,... | collective-permute-start | bytes 1179656 | tf_op jit(solution)/shard_map/ppermute | solution.py:276
  42.6 18.7 %collective-permute-start.11 = (f32[256,384]{1,0:T(8,128)S(1)}, f32[256,384]{1,0:T(8,128)S(1)}, u32[]{:S(2)}, u32[]{:S(2)}) collective-permute-start(f32[256,384]{1,0:T(8,128)S(1)} %add.78.refs_0_.held_ref), channel_id=1, source_target_pairs={{4,8},{5,9},{6,10},{7,11},{8,4},{9,5},{10,6},{11,7},{20,24},{21,25... | collective-permute-start | bytes 1179656 | tf_op jit(solution)/shard_map/ppermute | solution.py:276
  43.3 33.3 %collective-permute-start.6 = (f32[128,1280]{1,0:T(8,128)}, f32[128,1280]{1,0:T(8,128)S(1)}, u32[]{:S(2)}, u32[]{:S(2)}) collective-permute-start(f32[128,1280]{1,0:T(8,128)} %get-tuple-element.19), channel_id=1, source_target_pairs={{0,2},{1,3},{2,0},{3,1},{4,6},{5,7},{6,4},{7,5},{8,10},{9,11},{10,... | collective-permute-start | bytes 1966088 | tf_op jit(solution)/shard_map/ppermute | solution.py:276
  44.9 31.8 %collective-permute-start.7 = (f32[128,1280]{1,0:T(8,128)}, f32[128,1280]{1,0:T(8,128)S(1)}, u32[]{:S(2)}, u32[]{:S(2)}) collective-permute-start(f32[128,1280]{1,0:T(8,128)} %get-tuple-element.20), channel_id=1, source_target_pairs={{0,3},{1,2},{2,1},{3,0},{4,7},{5,6},{6,5},{7,4},{8,11},{9,10},{10,... | collective-permute-start | bytes 1966088 | tf_op jit(solution)/shard_map/ppermute | solution.py:276
  54.7 13.2 %collective-permute-start.15 = (f32[256,384]{1,0:T(8,128)}, f32[256,384]{1,0:T(8,128)}, u32[]{:S(2)}, u32[]{:S(2)}) collective-permute-start(f32[256,384]{1,0:T(8,128)} %plane_sum.10.refs_0_.held_ref), channel_id=1, source_target_pairs={{0,4},{1,5},{2,6},{3,7},{12,8},{13,9},{14,10},{15,11},{16,20},{17,... | collective-permute-start | bytes 1179656 | tf_op jit(solution)/shard_map/ppermute | solution.py:276
  61.3 12.7 %collective-permute-start.13 = (f32[256,384]{1,0:T(8,128)S(1)}, f32[256,384]{1,0:T(8,128)}, u32[]{:S(2)}, u32[]{:S(2)}) collective-permute-start(f32[256,384]{1,0:T(8,128)S(1)} %add.80.refs_0_.held_ref), channel_id=1, source_target_pairs={{4,0},{5,1},{6,2},{7,3},{8,12},{9,13},{10,14},{11,15},{20,16},{21,... | collective-permute-start | bytes 1179656 | tf_op jit(solution)/shard_map/ppermute | solution.py:276
  69.1 17.5 %collective-permute-start.19 = (f32[256,384]{1,0:T(8,128)S(1)}, f32[256,384]{1,0:T(8,128)S(1)}, u32[]{:S(2)}, u32[]{:S(2)}) collective-permute-start(f32[256,384]{1,0:T(8,128)S(1)} %add.81.refs_0_.held_ref), channel_id=1, source_target_pairs={{4,8},{5,9},{6,10},{7,11},{8,4},{9,5},{10,6},{11,7},{20,24},{21,25... | collective-permute-start | bytes 1179656 | tf_op jit(solution)/shard_map/ppermute | solution.py:276
  70.9 17.0 %collective-permute-start.18 = (f32[256,384]{1,0:T(8,128)S(1)}, f32[256,384]{1,0:T(8,128)S(1)}, u32[]{:S(2)}, u32[]{:S(2)}) collective-permute-start(f32[256,384]{1,0:T(8,128)S(1)} %add.82.refs_0_.held_ref), channel_id=1, source_target_pairs={{4,0},{5,1},{6,2},{7,3},{8,12},{9,13},{10,14},{11,15},{20,16},{21,... | collective-permute-start | bytes 1179656 | tf_op jit(solution)/shard_map/ppermute | solution.py:276
  75.0 13.5 %collective-permute-start.17 = (f32[256,384]{1,0:T(8,128)S(1)}, f32[256,384]{1,0:T(8,128)S(1)}, u32[]{:S(2)}, u32[]{:S(2)}) collective-permute-start(f32[256,384]{1,0:T(8,128)S(1)} %choose.8.refs_6_.refs_0_), channel_id=1, source_target_pairs={{0,2},{1,3},{2,0},{3,1},{4,6},{5,7},{6,4},{7,5},{8,10},{9,11},{10,... | collective-permute-start | bytes 1179656 | tf_op jit(solution)/shard_map/ppermute | solution.py:276
  78.0 15.0 %collective-permute-start.16 = (f32[256,384]{1,0:T(8,128)S(1)}, f32[256,384]{1,0:T(8,128)S(1)}, u32[]{:S(2)}, u32[]{:S(2)}) collective-permute-start(f32[256,384]{1,0:T(8,128)S(1)} %plane_sum.11.refs_6_.held_ref), channel_id=1, source_target_pairs={{0,4},{1,5},{2,6},{3,7},{12,8},{13,9},{14,10},{15,11},{16,20},{17,... | collective-permute-start | bytes 1179656 | tf_op jit(solution)/shard_map/ppermute | solution.py:276
  84.9 18.6 %collective-permute-start.21 = (f32[256,384]{1,0:T(8,128)S(1)}, f32[256,384]{1,0:T(8,128)S(1)}, u32[]{:S(2)}, u32[]{:S(2)}) collective-permute-start(f32[256,384]{1,0:T(8,128)S(1)} %plane_sum.12.refs_0_.held_ref), channel_id=1, source_target_pairs={{0,4},{1,5},{2,6},{3,7},{12,8},{13,9},{14,10},{15,11},{16,20},{17,... | collective-permute-start | bytes 1179656 | tf_op jit(solution)/shard_map/ppermute | solution.py:276
  86.6 14.5 %collective-permute-start.23 = (f32[256,384]{1,0:T(8,128)S(1)}, f32[256,384]{1,0:T(8,128)S(1)}, u32[]{:S(2)}, u32[]{:S(2)}) collective-permute-start(f32[256,384]{1,0:T(8,128)S(1)} %add.83.refs_0_.held_ref), channel_id=1, source_target_pairs={{4,0},{5,1},{6,2},{7,3},{8,12},{9,13},{10,14},{11,15},{20,16},{21,... | collective-permute-start | bytes 1179656 | tf_op jit(solution)/shard_map/ppermute | solution.py:276
  88.0 13.8 %collective-permute-start.22 = (f32[256,384]{1,0:T(8,128)S(1)}, f32[256,384]{1,0:T(8,128)S(1)}, u32[]{:S(2)}, u32[]{:S(2)}) collective-permute-start(f32[256,384]{1,0:T(8,128)S(1)} %choose.9.refs_2_.refs_0_), channel_id=1, source_target_pairs={{0,2},{1,3},{2,0},{3,1},{4,6},{5,7},{6,4},{7,5},{8,10},{9,11},{10,... | collective-permute-start | bytes 1179656 | tf_op jit(solution)/shard_map/ppermute | solution.py:276
  95.0 18.3 %collective-permute-start.27 = (f32[256,384]{1,0:T(8,128)S(1)}, f32[256,384]{1,0:T(8,128)S(1)}, u32[]{:S(2)}, u32[]{:S(2)}) collective-permute-start(f32[256,384]{1,0:T(8,128)S(1)} %plane_sum.13.refs_0_.held_ref), channel_id=1, source_target_pairs={{0,4},{1,5},{2,6},{3,7},{12,8},{13,9},{14,10},{15,11},{16,20},{17,... | collective-permute-start | bytes 1179656 | tf_op jit(solution)/shard_map/ppermute | solution.py:276
  113.4 13.4 %collective-permute-start.33 = (f32[256,384]{1,0:T(8,128)S(1)}, f32[256,384]{1,0:T(8,128)S(1)}, u32[]{:S(2)}, u32[]{:S(2)}) collective-permute-start(f32[256,384]{1,0:T(8,128)S(1)} %add.87.refs_0_.held_ref), channel_id=1, source_target_pairs={{4,8},{5,9},{6,10},{7,11},{8,4},{9,5},{10,6},{11,7},{20,24},{21,25... | collective-permute-start | bytes 1179656 | tf_op jit(solution)/shard_map/ppermute | solution.py:276
  114.1 14.0 %collective-permute-start.32 = (f32[256,384]{1,0:T(8,128)S(1)}, f32[256,384]{1,0:T(8,128)S(1)}, u32[]{:S(2)}, u32[]{:S(2)}) collective-permute-start(f32[256,384]{1,0:T(8,128)S(1)} %add.88.refs_0_.held_ref), channel_id=1, source_target_pairs={{4,0},{5,1},{6,2},{7,3},{8,12},{9,13},{10,14},{11,15},{20,16},{21,... | collective-permute-start | bytes 1179656 | tf_op jit(solution)/shard_map/ppermute | solution.py:276
  115.7 13.4 %collective-permute-start.31 = (f32[256,384]{1,0:T(8,128)S(1)}, f32[256,384]{1,0:T(8,128)S(1)}, u32[]{:S(2)}, u32[]{:S(2)}) collective-permute-start(f32[256,384]{1,0:T(8,128)S(1)} %choose.11.refs_0_), channel_id=1, source_target_pairs={{0,2},{1,3},{2,0},{3,1},{4,6},{5,7},{6,4},{7,5},{8,10},{9,11},{10,... | collective-permute-start | bytes 1179656 | tf_op jit(solution)/shard_map/ppermute | solution.py:276
  117.3 13.5 %collective-permute-start.30 = (f32[256,384]{1,0:T(8,128)S(1)}, f32[256,384]{1,0:T(8,128)S(1)}, u32[]{:S(2)}, u32[]{:S(2)}) collective-permute-start(f32[256,384]{1,0:T(8,128)S(1)} %add.89.refs_6_.held_ref), channel_id=1, source_target_pairs={{4,8},{5,9},{6,10},{7,11},{8,4},{9,5},{10,6},{11,7},{20,24},{21,25... | collective-permute-start | bytes 1179656 | tf_op jit(solution)/shard_map/ppermute | solution.py:276
  119.3 12.9 %collective-permute-start.29 = (f32[256,384]{1,0:T(8,128)S(1)}, f32[256,384]{1,0:T(8,128)S(1)}, u32[]{:S(2)}, u32[]{:S(2)}) collective-permute-start(f32[256,384]{1,0:T(8,128)S(1)} %plane_sum.15.refs_0_.held_ref), channel_id=1, source_target_pairs={{0,4},{1,5},{2,6},{3,7},{12,8},{13,9},{14,10},{15,11},{16,20},{17,... | collective-permute-start | bytes 1179656 | tf_op jit(solution)/shard_map/ppermute | solution.py:276
  130.9 13.4 %collective-permute-start.35 = (f32[256,384]{1,0:T(8,128)S(1)}, f32[256,384]{1,0:T(8,128)S(1)}, u32[]{:S(2)}, u32[]{:S(2)}) collective-permute-start(f32[256,384]{1,0:T(8,128)S(1)} %add.91.refs_0_.held_ref), channel_id=1, source_target_pairs={{4,0},{5,1},{6,2},{7,3},{8,12},{9,13},{10,14},{11,15},{20,16},{21,... | collective-permute-start | bytes 1179656 | tf_op jit(solution)/shard_map/ppermute | solution.py:276
  (30 other events, 274.7 us)

commit v3 on v2

--- a/solution.py
+++ b/solution.py
@@ -9,9 +9,9 @@
 CORES = 2
 PARTS = [2, 2, 2, 2, 2, 2, 2, 2]
 GROUPS = [[0], [1, 2], [3, 4, 5, 6, 7]]
-JOINED = []
-COSTS = [500000000, 500000000, 500000000, 1, 1, 500000000, 2000000000]
-ORDER = "m0 m1 0.0 m2 rs 1.0 rw 0.1 1.1 2.0 0.2 2.1 1.2 0.3 3.0 4.0 2.2 1.3 0.4 3.1 5.0 2.3 1.4 4.1 3.2 6.0 2.4 5.1 4.2 3.3 6.1 7.0 5.2 4.3 3.4 6.2 7.1 5.3 4.4 6.3 7.2 5.4 6.4 7.3 7.4"
+COSTS = [500000000, 500000000, 500000000, 1, 1, 500000000, 2000000000, 100000000000]
+SEND_RECOVERY, WAIT_RECOVERY = 100, 101
+ORDER = [-1, -2, 0, 10, 1, 100, 11, 20, -3, 101, 2, 21, 12, 3, 30, 40, 22, 13, 4, 31, 50, 23, 14, 41, 32, 60, 24, 51, 42, 33, 61, 70, 52, 43, 34, 62, 71, 53, 44, 63, 72, 54, 64, 73, 74]
 
 epsilon = 1e-06
 
@@ -19,6 +19,7 @@
 ANYWHERE = pl.BlockSpec(memory_space=pl.ANY)
 
 
+SCALARS = pl.BlockSpec(memory_space=pltpu.SMEM)
 PARAMS = pltpu.CompilerParams(vmem_limit_bytes=16 * 1024 * 1024)
 
 
@@ -52,17 +53,17 @@
         copy.wait()
 
 
-def cut(source, at, cuts, after=()):
+def cut(source, at, cuts, after=(), kind=5):
     def kernel(at_ref, source_ref, *refs):
         cut_kernel(cuts, at_ref, source_ref, *refs[len(after) :])
 
     return pl.pallas_call(
         kernel,
         out_shape=[jax.ShapeDtypeStruct((source.shape[0], size), source.dtype) for _, _, size in cuts],
-        in_specs=[pl.BlockSpec(memory_space=pltpu.SMEM), ANYWHERE] + [ANYWHERE] * len(after),
+        in_specs=[SCALARS, ANYWHERE] + [ANYWHERE] * len(after),
         out_specs=[ANYWHERE] * len(cuts),
         scratch_shapes=[pltpu.SemaphoreType.DMA((len(cuts),))],
-        cost_estimate=cost(5),
+        cost_estimate=cost(kind),
         compiler_params=PARAMS,
         name="cut_columns",
     )(at, source, *after)
@@ -116,7 +117,7 @@
     return pl.pallas_call(
         kernel,
         out_shape=jax.ShapeDtypeStruct((size, width), jnp.float32),
-        in_specs=[pl.BlockSpec(memory_space=pltpu.SMEM), ANYWHERE]
+        in_specs=[SCALARS, ANYWHERE]
         + [ANYWHERE] * len(maps)
         + [VMEM] * pairs
         + [ANYWHERE] * len(after),
@@ -146,33 +147,27 @@
     )(held, got, *after)
 
 
-def choose(takes, held, got, before, after):
-    above = before.shape[0] if before is not None else 0
-
+def choose(takes, held, got, after):
     def kernel(takes_ref, held_ref, got_ref, *refs):
         out = refs[-1]
-        if above:
-            out[:above] = refs[0][...]
 
         @pl.when(takes_ref[0] == 1)
         def _():
-            out[above:] = got_ref[...]
+            out[...] = got_ref[...]
 
         @pl.when(takes_ref[0] == 0)
         def _():
-            out[above:] = held_ref[...]
-
-    return pl.pallas_call(
-        kernel,
-        out_shape=jax.ShapeDtypeStruct((above + held.shape[0], held.shape[1]), held.dtype),
-        in_specs=[pl.BlockSpec(memory_space=pltpu.SMEM), VMEM, VMEM]
-        + [VMEM] * (above > 0)
-        + [ANYWHERE] * len(after),
+            out[...] = held_ref[...]
+
+    return pl.pallas_call(
+        kernel,
+        out_shape=jax.ShapeDtypeStruct(held.shape, held.dtype),
+        in_specs=[SCALARS, VMEM, VMEM] + [ANYWHERE] * len(after),
         out_specs=VMEM,
         cost_estimate=cost(3),
         compiler_params=PARAMS,
         name="choose",
-    )(takes, held, got, *([before] if above else []), *after)
+    )(takes, held, got, *after)
 
 
 def recover(at, recovery, recovery_got, begin, parts, total, after):
@@ -208,7 +203,7 @@
     return pl.pallas_call(
         kernel,
         out_shape=jax.ShapeDtypeStruct((rows, columns), jnp.float32),
-        in_specs=[pl.BlockSpec(memory_space=pltpu.SMEM), ANYWHERE, ANYWHERE]
+        in_specs=[SCALARS, ANYWHERE, ANYWHERE]
         + [VMEM] * count
         + [VMEM] * has_total
         + [ANYWHERE] * len(after),
@@ -297,15 +292,15 @@
     other_half = ((1 - core) * per_core).astype(jnp.int32).reshape(1)
 
     cuts = [(2, 0, per_lane)] + [(k, *span) for span in spans for k in (1, 3)]
-    pieces = list(cut(modal_map, at, cuts))
+    pieces = list(cut(modal_map, at, cuts, kind=7))
     map_from_core = send(pieces[0], OTHER_CORE)
     side_histories = send(histories, OTHER_SIDE)
     pieces = [pieces[1 + 2 * g : 3 + 2 * g] for g in range(len(GROUPS))]
     maps, held, flying = {}, {}, {}
     total, after, recovery_got, plane_histories = None, [], None, None
-    for work in ORDER.split():
-        if work[0] == "m":
-            g = int(work[1:])
+    for work in ORDER:
+        if work < 0:
+            g = -1 - work
             if g == 1:
                 joined = list(join([histories, side_histories], pieces[g], [map_from_core] + maps[0]))
                 pieces[g] = joined[1:]
@@ -313,14 +308,14 @@
                 after = joined[:1]
             maps[g] = [send(piece, pairs) for piece, pairs in zip(pieces[g], [OTHER_SIDE, OTHER_BOTH])]
             continue
-        if work == "rs":
+        if work == SEND_RECOVERY:
             after = list(cut(recovery, other_half, [(0, 0, per_core)], after))
             recovery_got = send(after[0], OTHER_CORE)
             continue
-        if work == "rw":
+        if work == WAIT_RECOVERY:
             after = after + [recovery_got]
             continue
-        i, step = (int(part) for part in work.split("."))
+        i, step = divmod(work, 10)
         if step == 0:
             side_map, both_map = maps[group_of[i]]
             begin = offsets[i] - spans[group_of[i]][0]
@@ -331,18 +326,14 @@
         elif step <= 2:
             value = add(held[i], flying[i], after)
         elif step == 3:
-            value = choose(outer, held[i], flying[i], held[i - 1] if i - 1 in JOINED else None, after)
-        elif i in JOINED:
-            continue
+            value = choose(outer, held[i], flying[i], after)
         else:
-            first = i - 1 if i - 1 in JOINED else i
             parts = [held[i], flying[i]]
-            value = total = recover(recovery_at, recovery, recovery_got, offsets[first], parts, total, after)
+            value = total = recover(recovery_at, recovery, recovery_got, offsets[i], parts, total, after)
         after = [value]
         if step < 4:
             held[i] = value
-            if step < 3 or i not in JOINED:
-                flying[i] = send(value, HOPS[step])
+            flying[i] = send(value, HOPS[step])
 
     rows = recovery.shape[0]
     return finish(total[:rows] + send(total[rows:], OTHER_CORE))

time: 169 us -> 168 us (level)
  starting transfers between devices: 69.5 us -> 67.7 us
    ppermute x43, starting transfers between devices: 69.5 us -> 67.7 us  [send(): return lax.ppermute(value, 'rows', pairs)]
where the time goes in v3:
time: 168 us; the launch traced here: 167 us
  starting transfers between devices  67.7 us (40%)
  waiting for transfers between devices  59.4 us (35%)
  Pallas kernels  32.8 us (20%)
  local copies, waits for them, and re-layouts  4.56 us (3%)
    ppermute x43, starting transfers between devices, send(): return lax.ppermute(value, 'rows', pairs)  67.7 us
    ppermute x43, waiting for transfers between devices, send(): return lax.ppermute(value, 'rows', pairs)  59.4 us
    pallas_call x8, Pallas kernels, recover(): pl.pallas_call(kernel, out_shape=jax.ShapeDtypeStruct((rows, columns), jn...  13.9 us
    pallas_call x8, Pallas kernels, plane_sum(): pl.pallas_call(kernel, out_shape=jax.ShapeDtypeStruct((size, width), jnp....  11.7 us
    unnamed x22, local copies, waits for them, and re-layouts  4.21 us
    pallas_call x16, Pallas kernels, add(): pl.pallas_call(kernel, out_shape=jax.ShapeDtypeStruct(held.shape, held.dt...  3.65 us
  transfers between devices with their start and end apart: 43, of which 16 were waited for; matrix products, arithmetic and copies ran while one was open for 0% of the time, Pallas kernels for 16%

profile of v3, /device:TPU:0, one launch (start us, length us, event | category | flops | bytes accessed | tf_op | source)
XLA Modules:
  0.0 167.4 jit_solution(3754430911358368643)
XLA Ops:
  0.8 2.2 %copy-done.2 = f32[128,8192]{1,0:T(8,128)S(1)} copy-done((f32[128,8192]{1,0:T(8,128)S(1)}, f32[128,8192]{1,0:T(8,128)}, u32[]{:S(2)}) %copy-start.2) | copy-done | bytes 4194328
  2.9 1.9 %cut_columns.2 = (f32[128,2048]{1,0:T(8,128)S(1)}, f32[128,256]{1,0:T(8,128)S(1)}, f32[128,256]{1,0:T(8,128)S(1)}, f32[128,512]{1,0:T(8,128)S(1)}, f32[128,512]{...) custom-call(s32[4]{0:T(128)S(1)} %pad_add_fusion.2.at_ref, f32[128,8192]{1,0:T(8,128)S(1)} %copy-done.2), custom_call_target="tpu_custom_call" | custom-call | flops 99999997952 | bytes 1 | tf_op jit(solution)/shard_map/cut_columns/pallas_call | solution.py:60
  5.4 2.6 %collective-permute-start.3 = (f32[128,384]{1,0:T(8,128)S(1)}, f32[128,384]{1,0:T(8,128)S(1)}, u32[]{:S(2)}, u32[]{:S(2)}) collective-permute-start(f32[128,384]{1,0:T(8,128)S(1)} %copy-done.5), channel_id=1, source_target_pairs={{0,2},{1,3},{2,0},{3,1},{4,6},{5,7},{6,4},{7,5},{8,10},{9,11},{10,... | collective-permute-start | bytes 589832 | tf_op jit(solution)/shard_map/ppermute | solution.py:271
  9.5 7.0 %collective-permute-done.refs_5_.refs_1_ = f32[128,256]{1,0:T(8,128)S(1)} collective-permute-done((f32[128,256]{1,0:T(8,128)S(1)}, f32[128,256]{1,0:T(8,128)S(1)}, u32[]{:S(2)}, u32[]{:S(2)}) %collective-permute-start) | collective-permute-done | bytes 131104 | tf_op jit(solution)/shard_map/ppermute | solution.py:271
  16.5 2.3 %collective-permute-done.2.refs_6_.refs_3_ = f32[128,256]{1,0:T(8,128)S(1)} collective-permute-done((f32[128,256]{1,0:T(8,128)S(1)}, f32[128,256]{1,0:T(8,128)S(1)}, u32[]{:S(2)}, u32[]{:S(2)}) %collective-permute-start.2) | collective-permute-done | bytes 131104 | tf_op jit(solution)/shard_map/ppermute | solution.py:271
  22.3 3.5 %collective-permute-start.5 = (f32[256,384]{1,0:T(8,128)S(1)}, f32[256,384]{1,0:T(8,128)S(1)}, u32[]{:S(2)}, u32[]{:S(2)}) collective-permute-start(f32[256,384]{1,0:T(8,128)S(1)} %plane_sum.8.refs_6_.held_ref), channel_id=1, source_target_pairs={{0,4},{1,5},{2,6},{3,7},{12,8},{13,9},{14,10},{15,11},{16,20},{17,... | collective-permute-start | bytes 1179656 | tf_op jit(solution)/shard_map/ppermute | solution.py:271
  27.4 7.6 %collective-permute-done.6.refs_1_ = f32[128,512]{1,0:T(8,128)S(1)} collective-permute-done((f32[128,512]{1,0:T(8,128)S(1)}, f32[128,512]{1,0:T(8,128)S(1)}, u32[]{:S(2)}, u32[]{:S(2)}) %collective-permute-start.6) | collective-permute-done | bytes 262176 | tf_op jit(solution)/shard_map/ppermute | solution.py:271
  35.1 3.7 %collective-permute-done.7.refs_3_ = f32[128,512]{1,0:T(8,128)S(1)} collective-permute-done((f32[128,512]{1,0:T(8,128)S(1)}, f32[128,512]{1,0:T(8,128)S(1)}, u32[]{:S(2)}, u32[]{:S(2)}) %collective-permute-start.7) | collective-permute-done | bytes 262176 | tf_op jit(solution)/shard_map/ppermute | solution.py:271
  45.4 6.2 %collective-permute-done.12.got_ref = f32[256,384]{1,0:T(8,128)S(1)} collective-permute-done((f32[256,384]{1,0:T(8,128)S(1)}, f32[256,384]{1,0:T(8,128)S(1)}, u32[]{:S(2)}, u32[]{:S(2)}) %collective-permute-start.12) | collective-permute-done | bytes 393248 | tf_op jit(solution)/shard_map/ppermute | solution.py:271
  52.4 2.1 %plane_sum.10.refs_0_.held_ref = f32[256,384]{1,0:T(8,128)} custom-call(s32[4]{0:T(128)S(1)} %pad_add_fusion.2.at_ref, f32[128,8192]{1,0:T(8,128)S(1)} %copy-done.3, f32[128,512]{1,0:T(8,128)S(1)} %collective-permute-done.6.refs_1_, f32[128,2048]{1,0:T(8,128)S(1)} %collective-permute-done.1.refs_4_.refs_2_, f32[128,512]{1,0:T(8,128)S(1)} %collective-permute-done.7.refs_3_, ...), custom_call_target="tpu_custom_call" | custom-call | flops 500000000 | bytes 1 | tf_op jit(solution)/shard_map/plane_sum/pallas_call | solution.py:117
  54.5 5.2 %collective-permute-start.15 = (f32[256,384]{1,0:T(8,128)}, f32[256,384]{1,0:T(8,128)}, u32[]{:S(2)}, u32[]{:S(2)}) collective-permute-start(f32[256,384]{1,0:T(8,128)} %plane_sum.10.refs_0_.held_ref), channel_id=1, source_target_pairs={{0,4},{1,5},{2,6},{3,7},{12,8},{13,9},{14,10},{15,11},{16,20},{17,... | collective-permute-start | bytes 1179656 | tf_op jit(solution)/shard_map/ppermute | solution.py:271
  61.1 2.0 %copy-done = f32[256,4096]{1,0:T(8,128)} copy-done((f32[256,4096]{1,0:T(8,128)}, f32[256,4096]{1,0:T(8,128)S(1)}, u32[]{:S(2)}) %copy-start) | copy-done | bytes 4194328
  64.4 2.5 %collective-permute-done.15.got_ref = f32[256,384]{1,0:T(8,128)} collective-permute-done((f32[256,384]{1,0:T(8,128)}, f32[256,384]{1,0:T(8,128)}, u32[]{:S(2)}, u32[]{:S(2)}) %collective-permute-start.15) | collective-permute-done | bytes 393248 | tf_op jit(solution)/shard_map/ppermute | solution.py:271
  71.2 3.8 %collective-permute-done.13.got_ref = f32[256,384]{1,0:T(8,128)} collective-permute-done((f32[256,384]{1,0:T(8,128)S(1)}, f32[256,384]{1,0:T(8,128)}, u32[]{:S(2)}, u32[]{:S(2)}) %collective-permute-start.13) | collective-permute-done | bytes 393248 | tf_op jit(solution)/shard_map/ppermute | solution.py:271
  79.0 3.5 %collective-permute-start.16 = (f32[256,384]{1,0:T(8,128)S(1)}, f32[256,384]{1,0:T(8,128)S(1)}, u32[]{:S(2)}, u32[]{:S(2)}) collective-permute-start(f32[256,384]{1,0:T(8,128)S(1)} %plane_sum.11.refs_6_.held_ref), channel_id=1, source_target_pairs={{0,4},{1,5},{2,6},{3,7},{12,8},{13,9},{14,10},{15,11},{16,20},{17,... | collective-permute-start | bytes 1179656 | tf_op jit(solution)/shard_map/ppermute | solution.py:271
  89.3 2.7 %collective-permute-done.16.got_ref = f32[256,384]{1,0:T(8,128)S(1)} collective-permute-done((f32[256,384]{1,0:T(8,128)S(1)}, f32[256,384]{1,0:T(8,128)S(1)}, u32[]{:S(2)}, u32[]{:S(2)}) %collective-permute-start.16) | collective-permute-done | bytes 393248 | tf_op jit(solution)/shard_map/ppermute | solution.py:271
  94.1 6.1 %collective-permute-start.27 = (f32[256,384]{1,0:T(8,128)S(1)}, f32[256,384]{1,0:T(8,128)S(1)}, u32[]{:S(2)}, u32[]{:S(2)}) collective-permute-start(f32[256,384]{1,0:T(8,128)S(1)} %plane_sum.13.refs_0_.held_ref), channel_id=1, source_target_pairs={{0,4},{1,5},{2,6},{3,7},{12,8},{13,9},{14,10},{15,11},{16,20},{17,... | collective-permute-start | bytes 1179656 | tf_op jit(solution)/shard_map/ppermute | solution.py:271
  106.0 4.7 %collective-permute-start.24 = (f32[256,384]{1,0:T(8,128)S(1)}, f32[256,384]{1,0:T(8,128)S(1)}, u32[]{:S(2)}, u32[]{:S(2)}) collective-permute-start(f32[256,384]{1,0:T(8,128)S(1)} %plane_sum.14.refs_3_.held_ref), channel_id=1, source_target_pairs={{0,4},{1,5},{2,6},{3,7},{12,8},{13,9},{14,10},{15,11},{16,20},{17,... | collective-permute-start | bytes 1179656 | tf_op jit(solution)/shard_map/ppermute | solution.py:271
  110.7 1.7 %recover.10.refs_0_.refs_2_ = f32[512,384]{1,0:T(8,128)S(1)} custom-call(s32[4]{0:T(128)S(1)} %pad_add_fusion.at_ref, f32[256,8192]{1,0:T(8,128)S(1)} %bitcast.16, f32[256,4096]{1,0:T(8,128)S(1)} %copy-done.1, f32[256,384]{1,0:T(8,128)S(1)} %choose.10.refs_3_.refs_0_, f32[256,384]{1,0:T(8,128)S(1)} %collective-permute-done.28.refs_1_, ...), custom_call_target="tpu_custom_call" | custom-call | flops 1 | bytes 1 | tf_op jit(solution)/shard_map/recover/pallas_call | solution.py:203
  118.3 7.4 %collective-permute-start.29 = (f32[256,384]{1,0:T(8,128)S(1)}, f32[256,384]{1,0:T(8,128)S(1)}, u32[]{:S(2)}, u32[]{:S(2)}) collective-permute-start(f32[256,384]{1,0:T(8,128)S(1)} %plane_sum.15.refs_0_.held_ref), channel_id=1, source_target_pairs={{0,4},{1,5},{2,6},{3,7},{12,8},{13,9},{14,10},{15,11},{16,20},{17,... | collective-permute-start | bytes 1179656 | tf_op jit(solution)/shard_map/ppermute | solution.py:271
  132.0 4.5 %collective-permute-done.37.got_ref = f32[256,384]{1,0:T(8,128)S(1)} collective-permute-done((f32[256,384]{1,0:T(8,128)S(1)}, f32[256,384]{1,0:T(8,128)S(1)}, u32[]{:S(2)}, u32[]{:S(2)}) %collective-permute-start.37) | collective-permute-done | bytes 393248 | tf_op jit(solution)/shard_map/ppermute | solution.py:271
  145.0 2.2 %collective-permute-done.40.refs_1_ = f32[256,384]{1,0:T(8,128)S(1)} collective-permute-done((f32[256,384]{1,0:T(8,128)S(1)}, f32[256,384]{1,0:T(8,128)S(1)}, u32[]{:S(2)}, u32[]{:S(2)}) %collective-permute-start.40) | collective-permute-done | bytes 393248 | tf_op jit(solution)/shard_map/ppermute | solution.py:271
  148.9 3.5 %collective-permute-done.39.refs_1_ = f32[256,384]{1,0:T(8,128)S(1)} collective-permute-done((f32[256,384]{1,0:T(8,128)S(1)}, f32[256,384]{1,0:T(8,128)S(1)}, u32[]{:S(2)}, u32[]{:S(2)}) %collective-permute-start.39) | collective-permute-done | bytes 393248 | tf_op jit(solution)/shard_map/ppermute | solution.py:271
  155.3 6.8 %collective-permute-done.41.refs_1_ = f32[256,384]{1,0:T(8,128)S(1)} collective-permute-done((f32[256,384]{1,0:T(8,128)S(1)}, f32[256,384]{1,0:T(8,128)S(1)}, u32[]{:S(2)}, u32[]{:S(2)}) %collective-permute-start.41) | collective-permute-done | bytes 393248 | tf_op jit(solution)/shard_map/ppermute | solution.py:271
  (139 shorter events, 70.3 us)
Async XLA Ops:
  4.8 14.0 %collective-permute-start.1 = (f32[128,2048]{1,0:T(8,128)S(1)}, f32[128,2048]{1,0:T(8,128)S(1)}, u32[]{:S(2)}, u32[]{:S(2)}) collective-permute-start(f32[128,2048]{1,0:T(8,128)S(1)} %get-tuple-element.14), channel_id=1, source_target_pairs={{0,1},{1,0},{2,3},{3,2},{4,5},{5,4},{6,7},{7,6},{8,9},{9,8},{10,11... | collective-permute-start | bytes 3145736 | tf_op jit(solution)/shard_map/ppermute | solution.py:271
  5.4 13.4 %collective-permute-start.3 = (f32[128,384]{1,0:T(8,128)S(1)}, f32[128,384]{1,0:T(8,128)S(1)}, u32[]{:S(2)}, u32[]{:S(2)}) collective-permute-start(f32[128,384]{1,0:T(8,128)S(1)} %copy-done.5), channel_id=1, source_target_pairs={{0,2},{1,3},{2,0},{3,1},{4,6},{5,7},{6,4},{7,5},{8,10},{9,11},{10,... | collective-permute-start | bytes 589832 | tf_op jit(solution)/shard_map/ppermute | solution.py:271
  22.3 17.8 %collective-permute-start.5 = (f32[256,384]{1,0:T(8,128)S(1)}, f32[256,384]{1,0:T(8,128)S(1)}, u32[]{:S(2)}, u32[]{:S(2)}) collective-permute-start(f32[256,384]{1,0:T(8,128)S(1)} %plane_sum.8.refs_6_.held_ref), channel_id=1, source_target_pairs={{0,4},{1,5},{2,6},{3,7},{12,8},{13,9},{14,10},{15,11},{16,20},{17,... | collective-permute-start | bytes 1179656 | tf_op jit(solution)/shard_map/ppermute | solution.py:271
  40.7 20.4 %collective-permute-start.8 = (f32[256,4096]{1,0:T(8,128)S(1)}, f32[256,4096]{1,0:T(8,128)S(1)}, u32[]{:S(2)}, u32[]{:S(2)}) collective-permute-start(f32[256,4096]{1,0:T(8,128)S(1)} %cut_columns.3.refs_0_), channel_id=1, source_target_pairs={{0,1},{1,0},{2,3},{3,2},{4,5},{5,4},{6,7},{7,6},{8,9},{9,8},{10,11... | collective-permute-start | bytes 12582920 | tf_op jit(solution)/shard_map/ppermute | solution.py:271
  43.1 16.6 %collective-permute-start.11 = (f32[256,384]{1,0:T(8,128)S(1)}, f32[256,384]{1,0:T(8,128)S(1)}, u32[]{:S(2)}, u32[]{:S(2)}) collective-permute-start(f32[256,384]{1,0:T(8,128)S(1)} %add.78.refs_0_.held_ref), channel_id=1, source_target_pairs={{4,8},{5,9},{6,10},{7,11},{8,4},{9,5},{10,6},{11,7},{20,24},{21,25... | collective-permute-start | bytes 1179656 | tf_op jit(solution)/shard_map/ppermute | solution.py:271
  43.8 33.9 %collective-permute-start.10 = (f32[128,1280]{1,0:T(8,128)}, f32[128,1280]{1,0:T(8,128)S(1)}, u32[]{:S(2)}, u32[]{:S(2)}) collective-permute-start(f32[128,1280]{1,0:T(8,128)} %get-tuple-element.22), channel_id=1, source_target_pairs={{0,3},{1,2},{2,1},{3,0},{4,7},{5,6},{6,5},{7,4},{8,11},{9,10},{10,... | collective-permute-start | bytes 1966088 | tf_op jit(solution)/shard_map/ppermute | solution.py:271
  44.7 32.9 %collective-permute-start.9 = (f32[128,1280]{1,0:T(8,128)}, f32[128,1280]{1,0:T(8,128)S(1)}, u32[]{:S(2)}, u32[]{:S(2)}) collective-permute-start(f32[128,1280]{1,0:T(8,128)} %get-tuple-element.21), channel_id=1, source_target_pairs={{0,2},{1,3},{2,0},{3,1},{4,6},{5,7},{6,4},{7,5},{8,10},{9,11},{10,... | collective-permute-start | bytes 1966088 | tf_op jit(solution)/shard_map/ppermute | solution.py:271
  54.5 12.4 %collective-permute-start.15 = (f32[256,384]{1,0:T(8,128)}, f32[256,384]{1,0:T(8,128)}, u32[]{:S(2)}, u32[]{:S(2)}) collective-permute-start(f32[256,384]{1,0:T(8,128)} %plane_sum.10.refs_0_.held_ref), channel_id=1, source_target_pairs={{0,4},{1,5},{2,6},{3,7},{12,8},{13,9},{14,10},{15,11},{16,20},{17,... | collective-permute-start | bytes 1179656 | tf_op jit(solution)/shard_map/ppermute | solution.py:271
  63.1 11.9 %collective-permute-start.13 = (f32[256,384]{1,0:T(8,128)S(1)}, f32[256,384]{1,0:T(8,128)}, u32[]{:S(2)}, u32[]{:S(2)}) collective-permute-start(f32[256,384]{1,0:T(8,128)S(1)} %add.80.refs_0_.held_ref), channel_id=1, source_target_pairs={{4,0},{5,1},{6,2},{7,3},{8,12},{9,13},{10,14},{11,15},{20,16},{21,... | collective-permute-start | bytes 1179656 | tf_op jit(solution)/shard_map/ppermute | solution.py:271
  68.1 17.5 %collective-permute-start.19 = (f32[256,384]{1,0:T(8,128)S(1)}, f32[256,384]{1,0:T(8,128)S(1)}, u32[]{:S(2)}, u32[]{:S(2)}) collective-permute-start(f32[256,384]{1,0:T(8,128)S(1)} %add.81.refs_0_.held_ref), channel_id=1, source_target_pairs={{4,8},{5,9},{6,10},{7,11},{8,4},{9,5},{10,6},{11,7},{20,24},{21,25... | collective-permute-start | bytes 1179656 | tf_op jit(solution)/shard_map/ppermute | solution.py:271
  69.9 17.0 %collective-permute-start.18 = (f32[256,384]{1,0:T(8,128)S(1)}, f32[256,384]{1,0:T(8,128)S(1)}, u32[]{:S(2)}, u32[]{:S(2)}) collective-permute-start(f32[256,384]{1,0:T(8,128)S(1)} %add.82.refs_0_.held_ref), channel_id=1, source_target_pairs={{4,0},{5,1},{6,2},{7,3},{8,12},{9,13},{10,14},{11,15},{20,16},{21,... | collective-permute-start | bytes 1179656 | tf_op jit(solution)/shard_map/ppermute | solution.py:271
  79.0 13.0 %collective-permute-start.16 = (f32[256,384]{1,0:T(8,128)S(1)}, f32[256,384]{1,0:T(8,128)S(1)}, u32[]{:S(2)}, u32[]{:S(2)}) collective-permute-start(f32[256,384]{1,0:T(8,128)S(1)} %plane_sum.11.refs_6_.held_ref), channel_id=1, source_target_pairs={{0,4},{1,5},{2,6},{3,7},{12,8},{13,9},{14,10},{15,11},{16,20},{17,... | collective-permute-start | bytes 1179656 | tf_op jit(solution)/shard_map/ppermute | solution.py:271
  83.9 18.6 %collective-permute-start.21 = (f32[256,384]{1,0:T(8,128)S(1)}, f32[256,384]{1,0:T(8,128)S(1)}, u32[]{:S(2)}, u32[]{:S(2)}) collective-permute-start(f32[256,384]{1,0:T(8,128)S(1)} %plane_sum.12.refs_0_.held_ref), channel_id=1, source_target_pairs={{0,4},{1,5},{2,6},{3,7},{12,8},{13,9},{14,10},{15,11},{16,20},{17,... | collective-permute-start | bytes 1179656 | tf_op jit(solution)/shard_map/ppermute | solution.py:271
  85.6 14.5 %collective-permute-start.23 = (f32[256,384]{1,0:T(8,128)S(1)}, f32[256,384]{1,0:T(8,128)S(1)}, u32[]{:S(2)}, u32[]{:S(2)}) collective-permute-start(f32[256,384]{1,0:T(8,128)S(1)} %add.83.refs_0_.held_ref), channel_id=1, source_target_pairs={{4,0},{5,1},{6,2},{7,3},{8,12},{9,13},{10,14},{11,15},{20,16},{21,... | collective-permute-start | bytes 1179656 | tf_op jit(solution)/shard_map/ppermute | solution.py:271
  87.0 13.8 %collective-permute-start.22 = (f32[256,384]{1,0:T(8,128)S(1)}, f32[256,384]{1,0:T(8,128)S(1)}, u32[]{:S(2)}, u32[]{:S(2)}) collective-permute-start(f32[256,384]{1,0:T(8,128)S(1)} %choose.9.refs_2_.refs_0_), channel_id=1, source_target_pairs={{0,2},{1,3},{2,0},{3,1},{4,6},{5,7},{6,4},{7,5},{8,10},{9,11},{10,... | collective-permute-start | bytes 1179656 | tf_op jit(solution)/shard_map/ppermute | solution.py:271
  94.1 18.4 %collective-permute-start.27 = (f32[256,384]{1,0:T(8,128)S(1)}, f32[256,384]{1,0:T(8,128)S(1)}, u32[]{:S(2)}, u32[]{:S(2)}) collective-permute-start(f32[256,384]{1,0:T(8,128)S(1)} %plane_sum.13.refs_0_.held_ref), channel_id=1, source_target_pairs={{0,4},{1,5},{2,6},{3,7},{12,8},{13,9},{14,10},{15,11},{16,20},{17,... | collective-permute-start | bytes 1179656 | tf_op jit(solution)/shard_map/ppermute | solution.py:271
  112.5 13.2 %collective-permute-start.33 = (f32[256,384]{1,0:T(8,128)S(1)}, f32[256,384]{1,0:T(8,128)S(1)}, u32[]{:S(2)}, u32[]{:S(2)}) collective-permute-start(f32[256,384]{1,0:T(8,128)S(1)} %add.87.refs_0_.held_ref), channel_id=1, source_target_pairs={{4,8},{5,9},{6,10},{7,11},{8,4},{9,5},{10,6},{11,7},{20,24},{21,25... | collective-permute-start | bytes 1179656 | tf_op jit(solution)/shard_map/ppermute | solution.py:271
  113.3 13.8 %collective-permute-start.32 = (f32[256,384]{1,0:T(8,128)S(1)}, f32[256,384]{1,0:T(8,128)S(1)}, u32[]{:S(2)}, u32[]{:S(2)}) collective-permute-start(f32[256,384]{1,0:T(8,128)S(1)} %add.88.refs_0_.held_ref), channel_id=1, source_target_pairs={{4,0},{5,1},{6,2},{7,3},{8,12},{9,13},{10,14},{11,15},{20,16},{21,... | collective-permute-start | bytes 1179656 | tf_op jit(solution)/shard_map/ppermute | solution.py:271
  114.8 13.3 %collective-permute-start.31 = (f32[256,384]{1,0:T(8,128)S(1)}, f32[256,384]{1,0:T(8,128)S(1)}, u32[]{:S(2)}, u32[]{:S(2)}) collective-permute-start(f32[256,384]{1,0:T(8,128)S(1)} %choose.11.refs_0_), channel_id=1, source_target_pairs={{0,2},{1,3},{2,0},{3,1},{4,6},{5,7},{6,4},{7,5},{8,10},{9,11},{10,... | collective-permute-start | bytes 1179656 | tf_op jit(solution)/shard_map/ppermute | solution.py:271
  116.3 13.5 %collective-permute-start.30 = (f32[256,384]{1,0:T(8,128)S(1)}, f32[256,384]{1,0:T(8,128)S(1)}, u32[]{:S(2)}, u32[]{:S(2)}) collective-permute-start(f32[256,384]{1,0:T(8,128)S(1)} %add.89.refs_6_.held_ref), channel_id=1, source_target_pairs={{4,8},{5,9},{6,10},{7,11},{8,4},{9,5},{10,6},{11,7},{20,24},{21,25... | collective-permute-start | bytes 1179656 | tf_op jit(solution)/shard_map/ppermute | solution.py:271
  118.3 12.9 %collective-permute-start.29 = (f32[256,384]{1,0:T(8,128)S(1)}, f32[256,384]{1,0:T(8,128)S(1)}, u32[]{:S(2)}, u32[]{:S(2)}) collective-permute-start(f32[256,384]{1,0:T(8,128)S(1)} %plane_sum.15.refs_0_.held_ref), channel_id=1, source_target_pairs={{0,4},{1,5},{2,6},{3,7},{12,8},{13,9},{14,10},{15,11},{16,20},{17,... | collective-permute-start | bytes 1179656 | tf_op jit(solution)/shard_map/ppermute | solution.py:271
  127.1 12.0 %collective-permute-start.36 = (f32[256,384]{1,0:T(8,128)S(1)}, f32[256,384]{1,0:T(8,128)S(1)}, u32[]{:S(2)}, u32[]{:S(2)}) collective-permute-start(f32[256,384]{1,0:T(8,128)S(1)} %choose.12.refs_3_.refs_0_), channel_id=1, source_target_pairs={{0,2},{1,3},{2,0},{3,1},{4,6},{5,7},{6,4},{7,5},{8,10},{9,11},{10,... | collective-permute-start | bytes 1179656 | tf_op jit(solution)/shard_map/ppermute | solution.py:271
  129.9 12.6 %collective-permute-start.35 = (f32[256,384]{1,0:T(8,128)S(1)}, f32[256,384]{1,0:T(8,128)S(1)}, u32[]{:S(2)}, u32[]{:S(2)}) collective-permute-start(f32[256,384]{1,0:T(8,128)S(1)} %add.91.refs_0_.held_ref), channel_id=1, source_target_pairs={{4,0},{5,1},{6,2},{7,3},{8,12},{9,13},{10,14},{11,15},{20,16},{21,... | collective-permute-start | bytes 1179656 | tf_op jit(solution)/shard_map/ppermute | solution.py:271
  131.3 12.4 %collective-permute-start.34 = (f32[256,384]{1,0:T(8,128)S(1)}, f32[256,384]{1,0:T(8,128)S(1)}, u32[]{:S(2)}, u32[]{:S(2)}) collective-permute-start(f32[256,384]{1,0:T(8,128)S(1)} %add.92.refs_0_.held_ref), channel_id=1, source_target_pairs={{4,8},{5,9},{6,10},{7,11},{8,4},{9,5},{10,6},{11,7},{20,24},{21,25... | collective-permute-start | bytes 1179656 | tf_op jit(solution)/shard_map/ppermute | solution.py:271
  (30 other events, 267.4 us)

commit v4 on v3

--- a/solution.py
+++ b/solution.py
@@ -9,7 +9,7 @@
 CORES = 2
 PARTS = [2, 2, 2, 2, 2, 2, 2, 2]
 GROUPS = [[0], [1, 2], [3, 4, 5, 6, 7]]
-COSTS = [500000000, 500000000, 500000000, 1, 1, 500000000, 2000000000, 100000000000]
+COSTS = {-1: 100000000000, -2: 2000000000, 0: 2000000000, 10: 20000000000, 3: 1, 4: 1, 13: 1, 14: 1, 23: 1, 24: 1, 33: 1, 34: 1, 43: 5000000000, 44: 1, 53: 1, 54: 1, 63: 1, 64: 1, 73: 1, 74: 1, 20: 20000000000, 11: 20000000000}
 SEND_RECOVERY, WAIT_RECOVERY = 100, 101
 ORDER = [-1, -2, 0, 10, 1, 100, 11, 20, -3, 101, 2, 21, 12, 3, 30, 40, 22, 13, 4, 31, 50, 23, 14, 41, 32, 60, 24, 51, 42, 33, 61, 70, 52, 43, 34, 62, 71, 53, 44, 63, 72, 54, 64, 73, 74]
 
@@ -24,7 +24,7 @@
 
 
 def cost(kind):
-    return pl.CostEstimate(flops=COSTS[kind], bytes_accessed=1, transcendentals=0)
+    return pl.CostEstimate(flops=COSTS.get(kind, 500000000), bytes_accessed=1, transcendentals=0)
 
 
 def halves(value):
@@ -53,7 +53,7 @@
         copy.wait()
 
 
-def cut(source, at, cuts, after=(), kind=5):
+def cut(source, at, cuts, after=(), kind=SEND_RECOVERY):
     def kernel(at_ref, source_ref, *refs):
         cut_kernel(cuts, at_ref, source_ref, *refs[len(after) :])
 
@@ -87,13 +87,13 @@
         in_specs=[VMEM] * count + [ANYWHERE] * (len(passed) + len(after)),
         out_specs=[VMEM] + [ANYWHERE] * len(passed),
         input_output_aliases={count + k: 1 + k for k in range(len(passed))},
-        cost_estimate=cost(6),
+        cost_estimate=cost(-2),
         compiler_params=PARAMS,
         name="join",
     )(*parts, *passed, *after)
 
 
-def plane_sum(at, modal_map, maps, histories, begin, past, size, after):
+def plane_sum(at, modal_map, maps, histories, begin, past, size, work, after):
     count = len(maps) + 1
     pairs = len(histories)
     depth, width = modal_map.shape[0], histories[0].shape[1]
@@ -126,13 +126,13 @@
             pltpu.VMEM((count * depth, size), jnp.float32),
             pltpu.SemaphoreType.DMA((count,)),
         ],
-        cost_estimate=cost(0),
+        cost_estimate=cost(work),
         compiler_params=PARAMS,
         name="plane_sum",
     )(at, modal_map, *maps, *histories, *after)
 
 
-def add(held, got, after):
+def add(held, got, work, after):
     def kernel(held_ref, got_ref, *refs):
         refs[-1][...] = held_ref[...] + got_ref[...]
 
@@ -141,13 +141,13 @@
         out_shape=jax.ShapeDtypeStruct(held.shape, held.dtype),
         in_specs=[VMEM, VMEM] + [ANYWHERE] * len(after),
         out_specs=VMEM,
-        cost_estimate=cost(1),
+        cost_estimate=cost(work),
         compiler_params=PARAMS,
         name="add",
     )(held, got, *after)
 
 
-def choose(takes, held, got, after):
+def choose(takes, held, got, work, after):
     def kernel(takes_ref, held_ref, got_ref, *refs):
         out = refs[-1]
 
@@ -164,13 +164,13 @@
         out_shape=jax.ShapeDtypeStruct(held.shape, held.dtype),
         in_specs=[SCALARS, VMEM, VMEM] + [ANYWHERE] * len(after),
         out_specs=VMEM,
-        cost_estimate=cost(3),
+        cost_estimate=cost(work),
         compiler_params=PARAMS,
         name="choose",
     )(takes, held, got, *after)
 
 
-def recover(at, recovery, recovery_got, begin, parts, total, after):
+def recover(at, recovery, recovery_got, begin, parts, total, work, after):
     size = parts[0].shape[0]
     count = len(parts)
     mine = recovery.shape[0]
@@ -209,7 +209,7 @@
         + [ANYWHERE] * len(after),
         out_specs=VMEM,
         scratch_shapes=[pltpu.VMEM((rows, count * size), jnp.float32), pltpu.SemaphoreType.DMA((sources,))],
-        cost_estimate=cost(4),
+        cost_estimate=cost(work),
         compiler_params=PARAMS,
         name="recover",
     )(at, recovery, recovery_got, *parts, *([total] if has_total else []), *after)
@@ -292,7 +292,7 @@
     other_half = ((1 - core) * per_core).astype(jnp.int32).reshape(1)
 
     cuts = [(2, 0, per_lane)] + [(k, *span) for span in spans for k in (1, 3)]
-    pieces = list(cut(modal_map, at, cuts, kind=7))
+    pieces = list(cut(modal_map, at, cuts, kind=-1))
     map_from_core = send(pieces[0], OTHER_CORE)
     side_histories = send(histories, OTHER_SIDE)
     pieces = [pieces[1 + 2 * g : 3 + 2 * g] for g in range(len(GROUPS))]
@@ -321,15 +321,15 @@
             begin = offsets[i] - spans[group_of[i]][0]
             value = plane_sum(
                 at, modal_map, [side_map, map_from_core, both_map], plane_histories,
-                offsets[i], [begin, offsets[i], begin], sizes[i], after,
+                offsets[i], [begin, offsets[i], begin], sizes[i], work, after,
             )
         elif step <= 2:
-            value = add(held[i], flying[i], after)
+            value = add(held[i], flying[i], work, after)
         elif step == 3:
-            value = choose(outer, held[i], flying[i], after)
+            value = choose(outer, held[i], flying[i], work, after)
         else:
             parts = [held[i], flying[i]]
-            value = total = recover(recovery_at, recovery, recovery_got, offsets[i], parts, total, after)
+            value = total = recover(recovery_at, recovery, recovery_got, offsets[i], parts, total, work, after)
         after = [value]
         if step < 4:
             held[i] = value

time: 168 us -> 166 us (0.988)
  waiting for transfers between devices: 59.4 us -> 51.1 us
  starting transfers between devices: 67.7 us -> 73.4 us
    ppermute x43, waiting for transfers between devices: 59.4 us -> 51.1 us  [send(): return lax.ppermute(value, 'rows', pairs)]
    ppermute x43, starting transfers between devices: 67.7 us -> 73.4 us  [send(): return lax.ppermute(value, 'rows', pairs)]
    unnamed x22 -> x24, local copies, waits for them, and re-layouts: 4.21 us -> 4.43 us
  transfers between devices with their start and end apart: 43 -> 43, of which waited for: 16 -> 14; matrix products, arithmetic and copies ran while one was open for 0% -> 0% of each run, Pallas kernels for 16% -> 18%
where the time goes in v4:
time: 166 us; the launch traced here: 165 us
  starting transfers between devices  73.4 us (44%)
  waiting for transfers between devices  51.1 us (31%)
  Pallas kernels  32.8 us (20%)
  local copies, waits for them, and re-layouts  4.78 us (3%)
    ppermute x43, starting transfers between devices, send(): return lax.ppermute(value, 'rows', pairs)  73.4 us
    ppermute x43, waiting for transfers between devices, send(): return lax.ppermute(value, 'rows', pairs)  51.1 us
    pallas_call x8, Pallas kernels, recover(): pl.pallas_call(kernel, out_shape=jax.ShapeDtypeStruct((rows, columns), jn...  13.9 us
    pallas_call x8, Pallas kernels, plane_sum(): pl.pallas_call(kernel, out_shape=jax.ShapeDtypeStruct((size, width), jnp....  10.9 us
    unnamed x24, local copies, waits for them, and re-layouts  4.43 us
  transfers between devices with their start and end apart: 43, of which 14 were waited for; matrix products, arithmetic and copies ran while one was open for 0% of the time, Pallas kernels for 18%

profile of v4, /device:TPU:0, one launch (start us, length us, event | category | flops | bytes accessed | tf_op | source)
XLA Modules:
  0.0 165.1 jit_solution(2335654827342855772)
XLA Ops:
  0.8 2.2 %copy-done.2 = f32[128,8192]{1,0:T(8,128)S(1)} copy-done((f32[128,8192]{1,0:T(8,128)S(1)}, f32[128,8192]{1,0:T(8,128)}, u32[]{:S(2)}) %copy-start.2) | copy-done | bytes 4194328
  2.9 1.9 %cut_columns.2 = (f32[128,2048]{1,0:T(8,128)S(1)}, f32[128,256]{1,0:T(8,128)S(1)}, f32[128,256]{1,0:T(8,128)S(1)}, f32[128,512]{1,0:T(8,128)S(1)}, f32[128,512]{...) custom-call(s32[4]{0:T(128)S(1)} %pad_add_fusion.2.at_ref, f32[128,8192]{1,0:T(8,128)S(1)} %copy-done.2), custom_call_target="tpu_custom_call" | custom-call | flops 99999997952 | bytes 1 | tf_op jit(solution)/shard_map/cut_columns/pallas_call | solution.py:60
  5.3 2.6 %collective-permute-start.3 = (f32[128,384]{1,0:T(8,128)S(1)}, f32[128,384]{1,0:T(8,128)S(1)}, u32[]{:S(2)}, u32[]{:S(2)}) collective-permute-start(f32[128,384]{1,0:T(8,128)S(1)} %copy-done.6), channel_id=1, source_target_pairs={{0,2},{1,3},{2,0},{3,1},{4,6},{5,7},{6,4},{7,5},{8,10},{9,11},{10,... | collective-permute-start | bytes 589832 | tf_op jit(solution)/shard_map/ppermute | solution.py:271
  9.5 7.0 %collective-permute-done.refs_5_.refs_1_ = f32[128,256]{1,0:T(8,128)S(1)} collective-permute-done((f32[128,256]{1,0:T(8,128)S(1)}, f32[128,256]{1,0:T(8,128)S(1)}, u32[]{:S(2)}, u32[]{:S(2)}) %collective-permute-start) | collective-permute-done | bytes 131104 | tf_op jit(solution)/shard_map/ppermute | solution.py:271
  16.5 2.3 %collective-permute-done.2.refs_6_.refs_3_ = f32[128,256]{1,0:T(8,128)S(1)} collective-permute-done((f32[128,256]{1,0:T(8,128)S(1)}, f32[128,256]{1,0:T(8,128)S(1)}, u32[]{:S(2)}, u32[]{:S(2)}) %collective-permute-start.2) | collective-permute-done | bytes 131104 | tf_op jit(solution)/shard_map/ppermute | solution.py:271
  22.4 3.8 %collective-permute-start.5 = (f32[256,384]{1,0:T(8,128)S(1)}, f32[256,384]{1,0:T(8,128)S(1)}, u32[]{:S(2)}, u32[]{:S(2)}) collective-permute-start(f32[256,384]{1,0:T(8,128)S(1)} %plane_sum.8.refs_6_.held_ref), channel_id=1, source_target_pairs={{0,4},{1,5},{2,6},{3,7},{12,8},{13,9},{14,10},{15,11},{16,20},{17,... | collective-permute-start | bytes 1179656 | tf_op jit(solution)/shard_map/ppermute | solution.py:271
  26.2 1.9 %collective-permute-done.6.refs_1_ = f32[128,512]{1,0:T(8,128)S(1)} collective-permute-done((f32[128,512]{1,0:T(8,128)S(1)}, f32[128,512]{1,0:T(8,128)S(1)}, u32[]{:S(2)}, u32[]{:S(2)}) %collective-permute-start.6) | collective-permute-done | bytes 262176 | tf_op jit(solution)/shard_map/ppermute | solution.py:271
  28.2 4.5 %collective-permute-done.7.refs_3_ = f32[128,512]{1,0:T(8,128)S(1)} collective-permute-done((f32[128,512]{1,0:T(8,128)S(1)}, f32[128,512]{1,0:T(8,128)S(1)}, u32[]{:S(2)}, u32[]{:S(2)}) %collective-permute-start.7) | collective-permute-done | bytes 262176 | tf_op jit(solution)/shard_map/ppermute | solution.py:271
  34.0 3.4 %collective-permute-start.12 = (f32[256,384]{1,0:T(8,128)S(1)}, f32[256,384]{1,0:T(8,128)S(1)}, u32[]{:S(2)}, u32[]{:S(2)}) collective-permute-start(f32[256,384]{1,0:T(8,128)S(1)} %plane_sum.9.refs_0_.held_ref), channel_id=1, source_target_pairs={{0,4},{1,5},{2,6},{3,7},{12,8},{13,9},{14,10},{15,11},{16,20},{17,... | collective-permute-start | bytes 1179656 | tf_op jit(solution)/shard_map/ppermute | solution.py:271
  41.0 5.8 %collective-permute-done.12.got_ref = f32[256,384]{1,0:T(8,128)S(1)} collective-permute-done((f32[256,384]{1,0:T(8,128)S(1)}, f32[256,384]{1,0:T(8,128)S(1)}, u32[]{:S(2)}, u32[]{:S(2)}) %collective-permute-start.12) | collective-permute-done | bytes 393248 | tf_op jit(solution)/shard_map/ppermute | solution.py:271
  48.1 4.4 %collective-permute-start.15 = (f32[256,384]{1,0:T(8,128)S(1)}, f32[256,384]{1,0:T(8,128)S(1)}, u32[]{:S(2)}, u32[]{:S(2)}) collective-permute-start(f32[256,384]{1,0:T(8,128)S(1)} %plane_sum.10.refs_0_.held_ref), channel_id=1, source_target_pairs={{0,4},{1,5},{2,6},{3,7},{12,8},{13,9},{14,10},{15,11},{16,20},{17,... | collective-permute-start | bytes 1179656 | tf_op jit(solution)/shard_map/ppermute | solution.py:271
  54.6 6.4 %collective-permute-done.15.got_ref = f32[256,384]{1,0:T(8,128)S(1)} collective-permute-done((f32[256,384]{1,0:T(8,128)S(1)}, f32[256,384]{1,0:T(8,128)S(1)}, u32[]{:S(2)}, u32[]{:S(2)}) %collective-permute-start.15) | collective-permute-done | bytes 393248 | tf_op jit(solution)/shard_map/ppermute | solution.py:271
  70.1 2.2 %copy-done.4 = f32[128,8192]{1,0:T(8,128)S(1)} copy-done((f32[128,8192]{1,0:T(8,128)S(1)}, f32[128,8192]{1,0:T(8,128)}, u32[]{:S(2)}) %copy-start.4) | copy-done | bytes 4194328
  73.7 5.3 %collective-permute-start.16 = (f32[256,384]{1,0:T(8,128)S(1)}, f32[256,384]{1,0:T(8,128)S(1)}, u32[]{:S(2)}, u32[]{:S(2)}) collective-permute-start(f32[256,384]{1,0:T(8,128)S(1)} %plane_sum.11.refs_6_.held_ref), channel_id=1, source_target_pairs={{0,4},{1,5},{2,6},{3,7},{12,8},{13,9},{14,10},{15,11},{16,20},{17,... | collective-permute-start | bytes 1179656 | tf_op jit(solution)/shard_map/ppermute | solution.py:271
  84.5 4.6 %collective-permute-start.21 = (f32[256,384]{1,0:T(8,128)S(1)}, f32[256,384]{1,0:T(8,128)S(1)}, u32[]{:S(2)}, u32[]{:S(2)}) collective-permute-start(f32[256,384]{1,0:T(8,128)S(1)} %plane_sum.12.refs_0_.held_ref), channel_id=1, source_target_pairs={{0,4},{1,5},{2,6},{3,7},{12,8},{13,9},{14,10},{15,11},{16,20},{17,... | collective-permute-start | bytes 1179656 | tf_op jit(solution)/shard_map/ppermute | solution.py:271
  93.1 3.0 %collective-permute-start.27 = (f32[256,384]{1,0:T(8,128)S(1)}, f32[256,384]{1,0:T(8,128)S(1)}, u32[]{:S(2)}, u32[]{:S(2)}) collective-permute-start(f32[256,384]{1,0:T(8,128)S(1)} %plane_sum.13.refs_0_.held_ref), channel_id=1, source_target_pairs={{0,4},{1,5},{2,6},{3,7},{12,8},{13,9},{14,10},{15,11},{16,20},{17,... | collective-permute-start | bytes 1179656 | tf_op jit(solution)/shard_map/ppermute | solution.py:271
  102.9 4.6 %collective-permute-start.24 = (f32[256,384]{1,0:T(8,128)S(1)}, f32[256,384]{1,0:T(8,128)S(1)}, u32[]{:S(2)}, u32[]{:S(2)}) collective-permute-start(f32[256,384]{1,0:T(8,128)S(1)} %plane_sum.14.refs_3_.held_ref), channel_id=1, source_target_pairs={{0,4},{1,5},{2,6},{3,7},{12,8},{13,9},{14,10},{15,11},{16,20},{17,... | collective-permute-start | bytes 1179656 | tf_op jit(solution)/shard_map/ppermute | solution.py:271
  114.8 7.2 %collective-permute-start.29 = (f32[256,384]{1,0:T(8,128)S(1)}, f32[256,384]{1,0:T(8,128)S(1)}, u32[]{:S(2)}, u32[]{:S(2)}) collective-permute-start(f32[256,384]{1,0:T(8,128)S(1)} %plane_sum.15.refs_0_.held_ref), channel_id=1, source_target_pairs={{0,4},{1,5},{2,6},{3,7},{12,8},{13,9},{14,10},{15,11},{16,20},{17,... | collective-permute-start | bytes 1179656 | tf_op jit(solution)/shard_map/ppermute | solution.py:271
  128.5 6.0 %collective-permute-done.37.got_ref = f32[256,384]{1,0:T(8,128)S(1)} collective-permute-done((f32[256,384]{1,0:T(8,128)S(1)}, f32[256,384]{1,0:T(8,128)S(1)}, u32[]{:S(2)}, u32[]{:S(2)}) %collective-permute-start.37) | collective-permute-done | bytes 393248 | tf_op jit(solution)/shard_map/ppermute | solution.py:271
  138.7 2.1 %collective-permute-start.39 = (f32[256,384]{1,0:T(8,128)S(1)}, f32[256,384]{1,0:T(8,128)S(1)}, u32[]{:S(2)}, u32[]{:S(2)}) collective-permute-start(f32[256,384]{1,0:T(8,128)S(1)} %choose.14.refs_0_), channel_id=1, source_target_pairs={{0,2},{1,3},{2,0},{3,1},{4,6},{5,7},{6,4},{7,5},{8,10},{9,11},{10,... | collective-permute-start | bytes 1179656 | tf_op jit(solution)/shard_map/ppermute | solution.py:271
  142.1 2.1 %collective-permute-done.40.refs_1_ = f32[256,384]{1,0:T(8,128)S(1)} collective-permute-done((f32[256,384]{1,0:T(8,128)S(1)}, f32[256,384]{1,0:T(8,128)S(1)}, u32[]{:S(2)}, u32[]{:S(2)}) %collective-permute-start.40) | collective-permute-done | bytes 393248 | tf_op jit(solution)/shard_map/ppermute | solution.py:271
  146.0 4.1 %collective-permute-done.39.refs_1_ = f32[256,384]{1,0:T(8,128)S(1)} collective-permute-done((f32[256,384]{1,0:T(8,128)S(1)}, f32[256,384]{1,0:T(8,128)S(1)}, u32[]{:S(2)}, u32[]{:S(2)}) %collective-permute-start.39) | collective-permute-done | bytes 393248 | tf_op jit(solution)/shard_map/ppermute | solution.py:271
  151.9 1.8 %collective-permute-start.41 = (f32[256,384]{1,0:T(8,128)S(1)}, f32[256,384]{1,0:T(8,128)S(1)}, u32[]{:S(2)}, u32[]{:S(2)}) collective-permute-start(f32[256,384]{1,0:T(8,128)S(1)} %choose.15.refs_0_.refs_3_), channel_id=1, source_target_pairs={{0,2},{1,3},{2,0},{3,1},{4,6},{5,7},{6,4},{7,5},{8,10},{9,11},{10,... | collective-permute-start | bytes 1179656 | tf_op jit(solution)/shard_map/ppermute | solution.py:271
  153.7 6.0 %collective-permute-done.41.refs_1_ = f32[256,384]{1,0:T(8,128)S(1)} collective-permute-done((f32[256,384]{1,0:T(8,128)S(1)}, f32[256,384]{1,0:T(8,128)S(1)}, u32[]{:S(2)}, u32[]{:S(2)}) %collective-permute-start.41) | collective-permute-done | bytes 393248 | tf_op jit(solution)/shard_map/ppermute | solution.py:271
  (141 shorter events, 68.4 us)
Async XLA Ops:
  4.8 14.0 %collective-permute-start.1 = (f32[128,2048]{1,0:T(8,128)S(1)}, f32[128,2048]{1,0:T(8,128)S(1)}, u32[]{:S(2)}, u32[]{:S(2)}) collective-permute-start(f32[128,2048]{1,0:T(8,128)S(1)} %get-tuple-element.14), channel_id=1, source_target_pairs={{0,1},{1,0},{2,3},{3,2},{4,5},{5,4},{6,7},{7,6},{8,9},{9,8},{10,11... | collective-permute-start | bytes 3145736 | tf_op jit(solution)/shard_map/ppermute | solution.py:271
  5.3 13.4 %collective-permute-start.3 = (f32[128,384]{1,0:T(8,128)S(1)}, f32[128,384]{1,0:T(8,128)S(1)}, u32[]{:S(2)}, u32[]{:S(2)}) collective-permute-start(f32[128,384]{1,0:T(8,128)S(1)} %copy-done.6), channel_id=1, source_target_pairs={{0,2},{1,3},{2,0},{3,1},{4,6},{5,7},{6,4},{7,5},{8,10},{9,11},{10,... | collective-permute-start | bytes 589832 | tf_op jit(solution)/shard_map/ppermute | solution.py:271
  22.4 15.0 %collective-permute-start.5 = (f32[256,384]{1,0:T(8,128)S(1)}, f32[256,384]{1,0:T(8,128)S(1)}, u32[]{:S(2)}, u32[]{:S(2)}) collective-permute-start(f32[256,384]{1,0:T(8,128)S(1)} %plane_sum.8.refs_6_.held_ref), channel_id=1, source_target_pairs={{0,4},{1,5},{2,6},{3,7},{12,8},{13,9},{14,10},{15,11},{16,20},{17,... | collective-permute-start | bytes 1179656 | tf_op jit(solution)/shard_map/ppermute | solution.py:271
  34.0 12.7 %collective-permute-start.12 = (f32[256,384]{1,0:T(8,128)S(1)}, f32[256,384]{1,0:T(8,128)S(1)}, u32[]{:S(2)}, u32[]{:S(2)}) collective-permute-start(f32[256,384]{1,0:T(8,128)S(1)} %plane_sum.9.refs_0_.held_ref), channel_id=1, source_target_pairs={{0,4},{1,5},{2,6},{3,7},{12,8},{13,9},{14,10},{15,11},{16,20},{17,... | collective-permute-start | bytes 1179656 | tf_op jit(solution)/shard_map/ppermute | solution.py:271
  38.0 15.3 %collective-permute-start.8 = (f32[256,4096]{1,0:T(8,128)S(1)}, f32[256,4096]{1,0:T(8,128)S(1)}, u32[]{:S(2)}, u32[]{:S(2)}) collective-permute-start(f32[256,4096]{1,0:T(8,128)S(1)} %cut_columns.3.refs_0_), channel_id=1, source_target_pairs={{0,1},{1,0},{2,3},{3,2},{4,5},{5,4},{6,7},{7,6},{8,9},{9,8},{10,11... | collective-permute-start | bytes 12582920 | tf_op jit(solution)/shard_map/ppermute | solution.py:271
  38.6 30.1 %collective-permute-start.10 = (f32[128,1280]{1,0:T(8,128)}, f32[128,1280]{1,0:T(8,128)S(1)}, u32[]{:S(2)}, u32[]{:S(2)}) collective-permute-start(f32[128,1280]{1,0:T(8,128)} %get-tuple-element.22), channel_id=1, source_target_pairs={{0,3},{1,2},{2,1},{3,0},{4,7},{5,6},{6,5},{7,4},{8,11},{9,10},{10,... | collective-permute-start | bytes 1966088 | tf_op jit(solution)/shard_map/ppermute | solution.py:271
  39.8 30.3 %collective-permute-start.9 = (f32[128,1280]{1,0:T(8,128)}, f32[128,1280]{1,0:T(8,128)S(1)}, u32[]{:S(2)}, u32[]{:S(2)}) collective-permute-start(f32[128,1280]{1,0:T(8,128)} %get-tuple-element.21), channel_id=1, source_target_pairs={{0,2},{1,3},{2,0},{3,1},{4,6},{5,7},{6,4},{7,5},{8,10},{9,11},{10,... | collective-permute-start | bytes 1966088 | tf_op jit(solution)/shard_map/ppermute | solution.py:271
  48.1 12.9 %collective-permute-start.15 = (f32[256,384]{1,0:T(8,128)S(1)}, f32[256,384]{1,0:T(8,128)S(1)}, u32[]{:S(2)}, u32[]{:S(2)}) collective-permute-start(f32[256,384]{1,0:T(8,128)S(1)} %plane_sum.10.refs_0_.held_ref), channel_id=1, source_target_pairs={{0,4},{1,5},{2,6},{3,7},{12,8},{13,9},{14,10},{15,11},{16,20},{17,... | collective-permute-start | bytes 1179656 | tf_op jit(solution)/shard_map/ppermute | solution.py:271
  53.3 12.7 %collective-permute-start.13 = (f32[256,384]{1,0:T(8,128)S(1)}, f32[256,384]{1,0:T(8,128)}, u32[]{:S(2)}, u32[]{:S(2)}) collective-permute-start(f32[256,384]{1,0:T(8,128)S(1)} %add.80.refs_0_.held_ref), channel_id=1, source_target_pairs={{4,0},{5,1},{6,2},{7,3},{8,12},{9,13},{10,14},{11,15},{20,16},{21,... | collective-permute-start | bytes 1179656 | tf_op jit(solution)/shard_map/ppermute | solution.py:271
  61.8 18.5 %collective-permute-start.19 = (f32[256,384]{1,0:T(8,128)}, f32[256,384]{1,0:T(8,128)}, u32[]{:S(2)}, u32[]{:S(2)}) collective-permute-start(f32[256,384]{1,0:T(8,128)} %add.81.refs_0_.held_ref), channel_id=1, source_target_pairs={{4,8},{5,9},{6,10},{7,11},{8,4},{9,5},{10,6},{11,7},{20,24},{21,25... | collective-permute-start | bytes 1179656 | tf_op jit(solution)/shard_map/ppermute | solution.py:271
  64.0 18.8 %collective-permute-start.18 = (f32[256,384]{1,0:T(8,128)}, f32[256,384]{1,0:T(8,128)}, u32[]{:S(2)}, u32[]{:S(2)}) collective-permute-start(f32[256,384]{1,0:T(8,128)} %add.82.refs_0_.held_ref), channel_id=1, source_target_pairs={{4,0},{5,1},{6,2},{7,3},{8,12},{9,13},{10,14},{11,15},{20,16},{21,... | collective-permute-start | bytes 1179656 | tf_op jit(solution)/shard_map/ppermute | solution.py:271
  67.1 22.1 %collective-permute-start.17 = (f32[256,384]{1,0:T(8,128)S(1)}, f32[256,384]{1,0:T(8,128)S(1)}, u32[]{:S(2)}, u32[]{:S(2)}) collective-permute-start(f32[256,384]{1,0:T(8,128)S(1)} %choose.8.refs_6_.refs_0_), channel_id=1, source_target_pairs={{0,2},{1,3},{2,0},{3,1},{4,6},{5,7},{6,4},{7,5},{8,10},{9,11},{10,... | collective-permute-start | bytes 1179656 | tf_op jit(solution)/shard_map/ppermute | solution.py:271
  73.7 17.3 %collective-permute-start.16 = (f32[256,384]{1,0:T(8,128)S(1)}, f32[256,384]{1,0:T(8,128)S(1)}, u32[]{:S(2)}, u32[]{:S(2)}) collective-permute-start(f32[256,384]{1,0:T(8,128)S(1)} %plane_sum.11.refs_6_.held_ref), channel_id=1, source_target_pairs={{0,4},{1,5},{2,6},{3,7},{12,8},{13,9},{14,10},{15,11},{16,20},{17,... | collective-permute-start | bytes 1179656 | tf_op jit(solution)/shard_map/ppermute | solution.py:271
  81.5 14.5 %collective-permute-start.23 = (f32[256,384]{1,0:T(8,128)S(1)}, f32[256,384]{1,0:T(8,128)S(1)}, u32[]{:S(2)}, u32[]{:S(2)}) collective-permute-start(f32[256,384]{1,0:T(8,128)S(1)} %add.83.refs_0_.held_ref), channel_id=1, source_target_pairs={{4,0},{5,1},{6,2},{7,3},{8,12},{9,13},{10,14},{11,15},{20,16},{21,... | collective-permute-start | bytes 1179656 | tf_op jit(solution)/shard_map/ppermute | solution.py:271
  83.9 13.7 %collective-permute-start.22 = (f32[256,384]{1,0:T(8,128)S(1)}, f32[256,384]{1,0:T(8,128)S(1)}, u32[]{:S(2)}, u32[]{:S(2)}) collective-permute-start(f32[256,384]{1,0:T(8,128)S(1)} %choose.9.refs_2_.refs_0_), channel_id=1, source_target_pairs={{0,2},{1,3},{2,0},{3,1},{4,6},{5,7},{6,4},{7,5},{8,10},{9,11},{10,... | collective-permute-start | bytes 1179656 | tf_op jit(solution)/shard_map/ppermute | solution.py:271
  84.5 14.9 %collective-permute-start.21 = (f32[256,384]{1,0:T(8,128)S(1)}, f32[256,384]{1,0:T(8,128)S(1)}, u32[]{:S(2)}, u32[]{:S(2)}) collective-permute-start(f32[256,384]{1,0:T(8,128)S(1)} %plane_sum.12.refs_0_.held_ref), channel_id=1, source_target_pairs={{0,4},{1,5},{2,6},{3,7},{12,8},{13,9},{14,10},{15,11},{16,20},{17,... | collective-permute-start | bytes 1179656 | tf_op jit(solution)/shard_map/ppermute | solution.py:271
  93.1 16.2 %collective-permute-start.27 = (f32[256,384]{1,0:T(8,128)S(1)}, f32[256,384]{1,0:T(8,128)S(1)}, u32[]{:S(2)}, u32[]{:S(2)}) collective-permute-start(f32[256,384]{1,0:T(8,128)S(1)} %plane_sum.13.refs_0_.held_ref), channel_id=1, source_target_pairs={{0,4},{1,5},{2,6},{3,7},{12,8},{13,9},{14,10},{15,11},{16,20},{17,... | collective-permute-start | bytes 1179656 | tf_op jit(solution)/shard_map/ppermute | solution.py:271
  109.3 12.7 %collective-permute-start.33 = (f32[256,384]{1,0:T(8,128)S(1)}, f32[256,384]{1,0:T(8,128)S(1)}, u32[]{:S(2)}, u32[]{:S(2)}) collective-permute-start(f32[256,384]{1,0:T(8,128)S(1)} %add.87.refs_0_.held_ref), channel_id=1, source_target_pairs={{4,8},{5,9},{6,10},{7,11},{8,4},{9,5},{10,6},{11,7},{20,24},{21,25... | collective-permute-start | bytes 1179656 | tf_op jit(solution)/shard_map/ppermute | solution.py:271
  110.0 13.3 %collective-permute-start.32 = (f32[256,384]{1,0:T(8,128)S(1)}, f32[256,384]{1,0:T(8,128)S(1)}, u32[]{:S(2)}, u32[]{:S(2)}) collective-permute-start(f32[256,384]{1,0:T(8,128)S(1)} %add.88.refs_0_.held_ref), channel_id=1, source_target_pairs={{4,0},{5,1},{6,2},{7,3},{8,12},{9,13},{10,14},{11,15},{20,16},{21,... | collective-permute-start | bytes 1179656 | tf_op jit(solution)/shard_map/ppermute | solution.py:271
  111.6 13.1 %collective-permute-start.31 = (f32[256,384]{1,0:T(8,128)S(1)}, f32[256,384]{1,0:T(8,128)S(1)}, u32[]{:S(2)}, u32[]{:S(2)}) collective-permute-start(f32[256,384]{1,0:T(8,128)S(1)} %choose.11.refs_0_), channel_id=1, source_target_pairs={{0,2},{1,3},{2,0},{3,1},{4,6},{5,7},{6,4},{7,5},{8,10},{9,11},{10,... | collective-permute-start | bytes 1179656 | tf_op jit(solution)/shard_map/ppermute | solution.py:271
  112.8 13.6 %collective-permute-start.30 = (f32[256,384]{1,0:T(8,128)S(1)}, f32[256,384]{1,0:T(8,128)S(1)}, u32[]{:S(2)}, u32[]{:S(2)}) collective-permute-start(f32[256,384]{1,0:T(8,128)S(1)} %add.89.refs_6_.held_ref), channel_id=1, source_target_pairs={{4,8},{5,9},{6,10},{7,11},{8,4},{9,5},{10,6},{11,7},{20,24},{21,25... | collective-permute-start | bytes 1179656 | tf_op jit(solution)/shard_map/ppermute | solution.py:271
  114.8 12.9 %collective-permute-start.29 = (f32[256,384]{1,0:T(8,128)S(1)}, f32[256,384]{1,0:T(8,128)S(1)}, u32[]{:S(2)}, u32[]{:S(2)}) collective-permute-start(f32[256,384]{1,0:T(8,128)S(1)} %plane_sum.15.refs_0_.held_ref), channel_id=1, source_target_pairs={{0,4},{1,5},{2,6},{3,7},{12,8},{13,9},{14,10},{15,11},{16,20},{17,... | collective-permute-start | bytes 1179656 | tf_op jit(solution)/shard_map/ppermute | solution.py:271
  123.4 12.6 %collective-permute-start.36 = (f32[256,384]{1,0:T(8,128)S(1)}, f32[256,384]{1,0:T(8,128)S(1)}, u32[]{:S(2)}, u32[]{:S(2)}) collective-permute-start(f32[256,384]{1,0:T(8,128)S(1)} %choose.12.refs_3_.refs_0_), channel_id=1, source_target_pairs={{0,2},{1,3},{2,0},{3,1},{4,6},{5,7},{6,4},{7,5},{8,10},{9,11},{10,... | collective-permute-start | bytes 1179656 | tf_op jit(solution)/shard_map/ppermute | solution.py:271
  127.8 13.0 %collective-permute-start.34 = (f32[256,384]{1,0:T(8,128)S(1)}, f32[256,384]{1,0:T(8,128)S(1)}, u32[]{:S(2)}, u32[]{:S(2)}) collective-permute-start(f32[256,384]{1,0:T(8,128)S(1)} %add.92.refs_0_.held_ref), channel_id=1, source_target_pairs={{4,8},{5,9},{6,10},{7,11},{8,4},{9,5},{10,6},{11,7},{20,24},{21,25... | collective-permute-start | bytes 1179656 | tf_op jit(solution)/shard_map/ppermute | solution.py:271
  (31 other events, 301.3 us)
